TPU v7x, 512 devices: a whole 4x8x8 slice. The times are simulated.
512 devices in a mesh: storage: 32 (over x, z), batch: 16 (over y, core).
Axes of the slice: x: 4, y: 8, z: 8, core: 2. Of those that a mesh axis runs over, the one named last changes fastest.
Arguments:
- node_features: bfloat16 [65536, 768], P(('storage', 'batch')), may hold values from -16 to 16
- history: float32 [65536, 768], P(('storage', 'batch')), may hold values from -6 to 6
- requests: int32 [16384, 8], P(('storage', 'batch')), may hold values from 0 to 127
- neighbours: int32 [65536, 16], P(('storage', 'batch')), may hold values from 0 to 255
- pattern: int32 [512, 16], P('storage'), may hold values from 0 to 1, as said below
- push_owner: int32 [65536], P(('storage', 'batch')), may hold values from 0 to 31, as said below
- push_slot: int32 [16384, 4], P(('storage', 'batch')), may hold values from 0 to 127, as said below
- w_query: bfloat16 [768, 384], replicated, may hold values from -1 to 1
- w_key: bfloat16 [768, 384], replicated, may hold values from -1 to 1
- w_value: bfloat16 [768, 384], replicated, may hold values from -0.21875 to 0.21875
- w_gate: bfloat16 [768, 384], replicated, may hold values from -0.21875 to 0.21875
- w_out: bfloat16 [384, 768], replicated, may hold values from -0.3125 to 0.3125
- cotangent: bfloat16 [65536, 768], P(('storage', 'batch')), may hold values from -0.75 to 0.75
Outputs:
- out_features: bfloat16 [65536, 768], P(('storage', 'batch'))
- new_history: float32 [65536, 768], P(('storage', 'batch'))
- grad_gate: float32 [768, 384], P('batch', 'storage')
- grad_value: float32 [768, 384], P('batch', 'storage')
Inputs may be any that keep to these rules, and one draw needn't show every extreme that they name: `pattern`: 0 or 1; every query block attends its own block. `push_owner`: exactly 4 nodes of each device name each storage index. `push_slot`: the 128 entries of one device are distinct.
All inputs are finite; a program needn't handle non-finite values.
Results may differ from a plain program's by a relative error of at most 0.035.
Values may be sent and summed in bfloat16 or wider, within the bound.
A program may use at most 64 MiB of HBM per device.

v0:
```python
import jax
import jax.numpy as jnp
from jax import lax
from jax.sharding import PartitionSpec as P

HEADS = 6
HEAD_DIM = 64
BLOCK = 128
NEIGHBOURS = 16


NEG = -1e30


def attention_scores(query_heads, key_heads, visible, inv_root):
    raw = (
        jnp.einsum("rhd,khd->hrk", query_heads, key_heads, preferred_element_type=jnp.float32)
        * inv_root
    )
    return jnp.where(visible[None], raw, NEG)


def on_device(
    node_features,
    history,
    requests,
    neighbours,
    pattern,
    push_owner,
    push_slot,
    w_query,
    w_key,
    w_value,
    w_gate,
    w_out,
    cotangent,
):
    n_store = lax.axis_size("storage")
    row_count = node_features.shape[0]
    model_width = node_features.shape[1]
    inv_root = HEAD_DIM ** (-0.5)
    position = lax.axis_index("batch")
    asked = lax.all_to_all(requests, "storage", split_axis=0, concat_axis=0, tiled=True)
    found = history[asked.reshape(-1)].astype(jnp.bfloat16)
    found = found.reshape(asked.shape[0], asked.shape[1], model_width)
    pulled = lax.all_to_all(found, "storage", split_axis=0, concat_axis=0, tiled=True)
    slot_total = pulled.shape[0] * pulled.shape[1]
    pulled_table = pulled.reshape(slot_total, model_width)
    counts = jnp.sum(
        (neighbours[:, :, None] == jnp.arange(slot_total, dtype=jnp.int32)[None, None, :]).astype(
            jnp.float32
        ),
        axis=1,
    ).astype(jnp.bfloat16)
    neighbour_mean = jnp.dot(counts, pulled_table, preferred_element_type=jnp.float32) / NEIGHBOURS
    hidden_in = (node_features.astype(jnp.float32) + neighbour_mean).astype(jnp.bfloat16)
    query_proj = jnp.dot(hidden_in, w_query, preferred_element_type=jnp.float32).astype(
        jnp.bfloat16
    )
    key_proj = jnp.dot(hidden_in, w_key, preferred_element_type=jnp.float32).astype(jnp.bfloat16)
    value_proj = jnp.dot(hidden_in, w_value, preferred_element_type=jnp.float32).astype(
        jnp.bfloat16
    )
    gate_proj = jnp.dot(hidden_in, w_gate, preferred_element_type=jnp.float32).astype(jnp.bfloat16)
    query_heads = query_proj.reshape(row_count, HEADS, HEAD_DIM)
    key_heads = key_proj.reshape(row_count, HEADS, HEAD_DIM)
    blocks_mine = row_count // BLOCK
    row_pattern = lax.dynamic_slice_in_dim(pattern, position * blocks_mine, blocks_mine, 0) > 0
    row_visible = jnp.repeat(jnp.repeat(row_pattern, BLOCK, axis=0), BLOCK, axis=1)
    column_pattern = lax.dynamic_slice_in_dim(pattern, position * blocks_mine, blocks_mine, 1) > 0
    column_visible = jnp.repeat(jnp.repeat(column_pattern, BLOCK, axis=0), BLOCK, axis=1)
    key_all, value_all = (
        lax.all_gather(key_proj, "batch", axis=0, tiled=True),
        lax.all_gather(value_proj, "batch", axis=0, tiled=True),
    )
    scores = attention_scores(
        query_heads, key_all.reshape(-1, HEADS, HEAD_DIM), row_visible, inv_root
    )
    row_max = lax.optimization_barrier(jnp.max(scores, axis=2).astype(jnp.bfloat16))
    raised = jnp.exp(scores - row_max.astype(jnp.float32)[:, :, None])
    row_sum = lax.optimization_barrier(jnp.sum(raised, axis=2).astype(jnp.bfloat16))
    weights = (raised / row_sum.astype(jnp.float32)[:, :, None]).astype(jnp.bfloat16)
    attended = jnp.einsum(
        "hrk,khd->rhd",
        weights,
        value_all.reshape(-1, HEADS, HEAD_DIM),
        preferred_element_type=jnp.float32,
    )
    attended = attended.astype(jnp.bfloat16).reshape(row_count, HEADS * HEAD_DIM)
    gated = (attended.astype(jnp.float32) * gate_proj.astype(jnp.float32)).astype(jnp.bfloat16)
    out_features = (
        node_features.astype(jnp.float32)
        + jnp.dot(gated, w_out, preferred_element_type=jnp.float32)
    ).astype(jnp.bfloat16)
    sorted_rows = jnp.argsort(push_owner, stable=True)
    sending = out_features[sorted_rows].reshape(n_store, row_count // n_store, model_width)
    arrived = lax.all_to_all(sending, "storage", split_axis=0, concat_axis=0, tiled=True)
    new_history = history.at[push_slot.reshape(-1)].set(
        arrived.reshape(-1, model_width).astype(jnp.float32)
    )
    back_gated = jnp.einsum(
        "rd,hd->rh", cotangent, w_out, preferred_element_type=jnp.float32
    ).astype(jnp.bfloat16)
    back_gate = (back_gated.astype(jnp.float32) * attended.astype(jnp.float32)).astype(jnp.bfloat16)
    back_attended = (back_gated.astype(jnp.float32) * gate_proj.astype(jnp.float32)).astype(
        jnp.bfloat16
    )
    grad_g = jnp.einsum("rd,rh->dh", hidden_in, back_gate, preferred_element_type=jnp.float32)
    query_in = lax.all_gather(query_proj, "batch", axis=0, tiled=True)
    back_in = lax.all_gather(back_attended, "batch", axis=0, tiled=True)
    max_in = lax.all_gather(row_max.T, "batch", axis=0, tiled=True)
    sum_in = lax.all_gather(row_sum.T, "batch", axis=0, tiled=True)
    arriving = query_in.shape[0]
    scores = attention_scores(
        query_in.reshape(arriving, HEADS, HEAD_DIM), key_heads, column_visible, inv_root
    )
    weights = (
        jnp.exp(scores - max_in.astype(jnp.float32).T[:, :, None])
        / sum_in.astype(jnp.float32).T[:, :, None]
    ).astype(jnp.bfloat16)
    back_values = jnp.einsum(
        "hqk,qhd->khd",
        weights,
        back_in.reshape(arriving, HEADS, HEAD_DIM),
        preferred_element_type=jnp.float32,
    )
    back_values = back_values.astype(jnp.bfloat16).reshape(row_count, HEADS * HEAD_DIM)
    grad_v = jnp.einsum("rd,rh->dh", hidden_in, back_values, preferred_element_type=jnp.float32)
    partial_sums = (
        lax.psum_scatter(
            grad_g.astype(jnp.bfloat16), "storage", scatter_dimension=1, tiled=True
        ).astype(jnp.float32),
        lax.psum_scatter(
            grad_v.astype(jnp.bfloat16), "storage", scatter_dimension=1, tiled=True
        ).astype(jnp.float32),
    )
    grad_gate, grad_value = (
        lax.psum_scatter(
            partial_sums[0].astype(jnp.bfloat16), "batch", scatter_dimension=0, tiled=True
        ).astype(jnp.float32),
        lax.psum_scatter(
            partial_sums[1].astype(jnp.bfloat16), "batch", scatter_dimension=0, tiled=True
        ).astype(jnp.float32),
    )
    return (out_features, new_history, grad_gate, grad_value)


def solution(mesh):
    in_specs = (
        P(("storage", "batch"), None),
        P(("storage", "batch"), None),
        P(("storage", "batch"), None),
        P(("storage", "batch"), None),
        P("storage", None),
        P(("storage", "batch")),
        P(("storage", "batch"), None),
        P(),
        P(),
        P(),
        P(),
        P(),
        P(("storage", "batch"), None),
    )
    out_specs = (
        P(("storage", "batch"), None),
        P(("storage", "batch"), None),
        P("batch", "storage"),
        P("batch", "storage"),
    )
    return jax.shard_map(
        on_device, mesh=mesh, in_specs=in_specs, out_specs=out_specs, check_vma=False
    )
```

profile of v0, /device:TPU:1, one launch (start us, length us, event | category | flops | bytes accessed | tf_op | source)
XLA Modules:
  0.0 509.3 jit_solution(8160839791151444880)
XLA Ops:
  7.2 1.1 copy.64
  9.1 22.1 %all_to_all.19 = s32[32,1,8]{2,1,0:T(1,128)S(1)} all-to-all(s32[32,1,8]{2,1,0:T(1,128)S(1)} %bitcast.71), channel_id=1, replica_groups=mesh['storage'=32,'batch'=16] {'storage'}, dimensions={0} | all-to-all | bytes 2048 | tf_op jit(solution)/shard_map/all_to_all | solution.py:43
  32.6 1.8 gather_fusion
  34.4 3.9 all-to-all-start.1
  39.8 9.0 %all-to-all-done.1 = bf16[32,8,768]{2,1,0:T(8,128)(2,1)S(1)} async-done(((bf16[32,8,768]{2,1,0:T(8,128)(2,1)}), bf16[32,8,768]{2,1,0:T(8,128)(2,1)S(1)}, u32[]{:S(2)}, u32[]{:S(2)}) %all-to-all-start.1) | async-done | bytes 393248 | tf_op jit(solution)/shard_map/all_to_all | solution.py:46
  52.2 1.9 multiply_convert_fusion
  54.5 2.0 convolution_convert_fusion.5
  56.6 2.5 sort.17
  60.1 1.6 copy.57
  61.7 32.2 %all-gather.7.cloned.1.call-done = bf16[2048,384]{1,0:T(8,128)(2,1)} async-done(((bf16[128,384]{1,0:T(8,128)(2,1)}), bf16[2048,384]{1,0:T(8,128)(2,1)}) %all-gather.7.cloned.1.call-update) | async-done | bytes 1572880 | tf_op jit(solution)/shard_map/all_gather | solution.py:73
  93.9 1.7 copy.51
  96.8 2.6 copy-done.2
  99.4 1.3 fusion.3
  100.8 36.4 %all-gather.5.cloned.1.call-done = bf16[2048,384]{1,0:T(8,128)(2,1)} async-done(((bf16[128,384]{1,0:T(8,128)(2,1)}), bf16[2048,384]{1,0:T(8,128)(2,1)}) %all-gather.5.cloned.1.call-update) | async-done | bytes 1572880 | tf_op jit(solution)/shard_map/all_gather | solution.py:74
  137.2 1.7 copy.49
  138.9 3.9 fusion.11
  142.9 37.0 %all-gather.9.cloned.1.call-done = bf16[2048,384]{1,0:T(8,128)(2,1)} async-done(((bf16[128,384]{1,0:T(8,128)(2,1)}), bf16[2048,384]{1,0:T(8,128)(2,1)}) %all-gather.9.cloned.1.call-update) | async-done | bytes 1572880 | tf_op jit(solution)/shard_map/all_gather | solution.py:110
  179.9 1.7 copy.55
  181.6 15.7 %all_gather.23 = bf16[2048,6]{0,1:T(8,128)(2,1)S(1)} all-gather(bf16[128,6]{0,1:T(8,128)(2,1)S(1)} %bitcast.73), channel_id=1, replica_groups=mesh['storage'=32,'batch'=16] {'batch'}, dimensions={0}, use_global_device_ids=true | all-gather | bytes 26112 | tf_op jit(solution)/shard_map/all_gather | solution.py:112
  197.3 15.0 %all_gather.22 = bf16[2048,6]{0,1:T(8,128)(2,1)S(1)} all-gather(bf16[128,6]{0,1:T(8,128)(2,1)S(1)} %bitcast.72), channel_id=1, replica_groups=mesh['storage'=32,'batch'=16] {'batch'}, dimensions={0}, use_global_device_ids=true | all-gather | bytes 26112 | tf_op jit(solution)/shard_map/all_gather | solution.py:111
  213.5 9.5 %all-gather.11.cloned.1.call-done = bf16[2048,384]{1,0:T(8,128)(2,1)} async-done(((bf16[128,384]{1,0:T(8,128)(2,1)}), bf16[2048,384]{1,0:T(8,128)(2,1)}) %all-gather.11.cloned.1.call-update) | async-done | bytes 1572880 | tf_op jit(solution)/shard_map/all_gather | solution.py:109
  223.0 2.6 copy.56
  225.6 6.8 %fusion.9 = bf16[6,64,128]{2,1,0:T(8,128)(2,1)} fusion(bf16[2048,6,64]{0,2,1:T(8,128)(2,1)S(1)} %bitcast.64, bf16[2048,6,64]{0,2,1:T(8,128)(2,1)} %bitcast.65, bf16[128,6,64]{0,2,1:T(8,128)(2,1)} %bitcast.70, f32[6,2048]{1,0:T(8,128)} %convert_bitcast_fusion.1, f32[6,2048]{1,0:T(8,128)} %convert_bitcast_fusion.2, pred[2048]{0:T(1024)(128)(4,1)S(1)} %broadcast_bitcast_fusion), kind=kOutput, calls=%fused_computation.20 | convolution fusion | flops 410566656 | bytes 3442688 | tf_op jit(solution)/shard_map/hqk,qhd->khd/dot_general | solution.py:121
  232.4 1.2 convolution_convert_fusion
  234.0 71.2 %fusion.22 = (bf16[768,16]{0,1:T(8,128)(2,1)S(1)}, bf16[768,16]{0,1:T(8,128)(2,1)S(1)}) fusion(bf16[768,384]{0,1:T(8,128)(2,1)S(1)} %convolution_convert_fusion.1, bf16[768,384]{0,1:T(8,128)(2,1)S(1)} %convolution_convert_fusion), kind=kCustom, calls=%all-reduce-scatter.2 | all-reduce-scatter fusion | flops 786433 | bytes 1230848
  305.2 1.3 collective-permute-start.15
  306.5 1.3 collective-permute-start.10
  307.8 1.3 collective-permute-start.11
  309.1 1.3 collective-permute-start.12
  310.4 4.6 collective-permute-start.13
  315.0 6.4 %collective-permute-start.14 = (bf16[768,16]{0,1:T(8,128)(2,1)S(1)}, bf16[768,16]{0,1:T(8,128)(2,1)S(1)}, u32[]{:S(2)}, u32[]{:S(2)}) collective-permute-start(bf16[768,16]{0,1:T(8,128)(2,1)S(1)} %get-tuple-element.9), channel_id=1, source_target_pairs={{0,112},{16,128},{32,144},{48,160},{64,176},{80,192},{96,208},{112... | collective-permute-start | bytes 73736
  321.7 1.3 dynamic-slice.6
  323.6 4.3 collective-permute-start.8
  328.0 1.9 collective-permute-start.9
  329.9 4.3 collective-permute-start
  334.2 3.4 collective-permute-start.1
  337.6 1.3 collective-permute-start.7
  340.8 3.9 all-to-all-start.2
  344.7 4.8 collective-permute-start.2
  349.5 4.3 collective-permute-start.3
  353.9 1.1 concatenate.1
  355.0 7.0 %collective-permute-start.4 = (bf16[768,16]{0,1:T(8,128)(2,1)S(1)}, bf16[768,16]{0,1:T(8,128)(2,1)S(1)}, u32[]{:S(2)}, u32[]{:S(2)}) collective-permute-start(bf16[768,16]{0,1:T(8,128)(2,1)S(1)} %get-tuple-element.8), channel_id=1, source_target_pairs={{0,80},{16,96},{32,112},{48,128},{64,144},{80,160},{96,176},{112,1... | collective-permute-start | bytes 73736
  362.1 3.1 collective-permute-start.5
  365.2 2.8 collective-permute-start.6
  369.1 1.1 concatenate
  371.1 67.7 %reduce-scatter.13.cloned.1.call-done = bf16[48,12]{1,0:T(8,128)(2,1)} async-done(((bf16[768,12]{1,0:T(8,128)(2,1)}), bf16[48,12]{1,0:T(8,128)(2,1)}) %reduce-scatter.13.cloned.1.call-update) | async-done | bytes 1168
  440.3 58.8 %reduce-scatter.11.cloned.1.call-done = bf16[48,12]{1,0:T(8,128)(2,1)} async-done(((bf16[768,12]{1,0:T(8,128)(2,1)}), bf16[48,12]{1,0:T(8,128)(2,1)}) %reduce-scatter.11.cloned.1.call-update) | async-done | bytes 1168
  500.5 1.2 scatter_fusion
  (94 shorter events, 18.7 us)
Async XLA Ops:
  7.2 45.1 %copy-start = (bf16[384,768]{1,0:T(8,128)(2,1)S(1)}, bf16[384,768]{1,0:T(8,128)(2,1)}, u32[]{:S(2)}) copy-start(bf16[384,768]{1,0:T(8,128)(2,1)} %param.24) | copy-start | bytes 1769476
  7.2 47.0 %copy-start.8 = (s32[16,16]{1,0:T(8,128)S(1)}, s32[16,16]{1,0:T(8,128)}, u32[]{:S(2)}) copy-start(s32[16,16]{1,0:T(8,128)} %param.17) | copy-start | bytes 3076
  7.2 49.4 %copy-start.10 = (s32[128]{0:T(128)S(1)}, s32[128]{0:T(128)}, u32[]{:S(2)}) copy-start(s32[128]{0:T(128)} %param.18) | copy-start | bytes 1540
  7.2 42.8 %copy-start.5 = (bf16[768,384]{1,0:T(8,128)(2,1)S(1)}, bf16[768,384]{1,0:T(8,128)(2,1)}, u32[]{:S(2)}) copy-start(bf16[768,384]{1,0:T(8,128)(2,1)} %param.21) | copy-start | bytes 1769476
  7.2 43.8 %copy-start.6 = (bf16[768,384]{1,0:T(8,128)(2,1)S(1)}, bf16[768,384]{1,0:T(8,128)(2,1)}, u32[]{:S(2)}) copy-start(bf16[768,384]{1,0:T(8,128)(2,1)} %param.22) | copy-start | bytes 1769476
  7.2 44.7 %copy-start.7 = (bf16[768,384]{1,0:T(8,128)(2,1)S(1)}, bf16[768,384]{1,0:T(8,128)(2,1)}, u32[]{:S(2)}) copy-start(bf16[768,384]{1,0:T(8,128)(2,1)} %param.23) | copy-start | bytes 1769476
  34.4 14.4 %all-to-all-start.1 = ((bf16[32,8,768]{2,1,0:T(8,128)(2,1)}), bf16[32,8,768]{2,1,0:T(8,128)(2,1)S(1)}, u32[]{:S(2)}, u32[]{:S(2)}) async-start(bf16[32,8,768]{2,1,0:T(8,128)(2,1)} %bitcast.40), calls=%async_computation.1 | async-start | bytes 786432 | tf_op jit(solution)/shard_map/all_to_all | solution.py:46
  38.3 55.6 %all-gather.7.cloned.1.call-start = ((), (), s32[]{:S(2)}) async-start(), calls=%async_computation.6 | async-start | bytes 1671168 | tf_op jit(solution)/shard_map/all_gather | solution.py:73
  50.9 86.2 %all-gather.5.cloned.1.call-start = ((), (), s32[]{:S(2)}) async-start(), calls=%async_computation.5 | async-start | bytes 1671168 | tf_op jit(solution)/shard_map/all_gather | solution.py:74
  51.9 127.9 %all-gather.9.cloned.1.call-start = ((), (), s32[]{:S(2)}) async-start(), calls=%async_computation.7 | async-start | bytes 1671168 | tf_op jit(solution)/shard_map/all_gather | solution.py:110
  54.2 168.8 %all-gather.11.cloned.1.call-start = ((), (), s32[]{:S(2)}) async-start(), calls=%async_computation.8 | async-start | bytes 1671168 | tf_op jit(solution)/shard_map/all_gather | solution.py:109
  96.7 2.7 copy-start.2
  225.6 95.9 %copy-start.9 = (s32[32,4]{0,1:T(4,128)S(1)}, s32[32,4]{0,1:T(4,128)}, u32[]{:S(2)}) copy-start(s32[32,4]{0,1:T(4,128)} %param.19) | copy-start | bytes 1540
  225.6 113.3 %copy-start.4 = (bf16[128,768]{1,0:T(8,128)(2,1)S(1)}, bf16[128,768]{1,0:T(8,128)(2,1)}, u32[]{:S(2)}) copy-start(bf16[128,768]{1,0:T(8,128)(2,1)} %param.13) | copy-start | bytes 589828
  305.2 9.8 %collective-permute-start.15 = (bf16[768,12]{0,1:T(8,128)(2,1)S(1)}, bf16[768,12]{0,1:T(8,128)(2,1)S(1)}, u32[]{:S(2)}, u32[]{:S(2)}) collective-permute-start(bf16[768,12]{0,1:T(8,128)(2,1)S(1)} %slice.5), channel_id=1, source_target_pairs={{0,128},{16,144},{32,160},{48,176},{64,192},{80,208},{96,224},{112... | collective-permute-start | bytes 55304
  306.5 17.1 %collective-permute-start.10 = (bf16[768,16]{0,1:T(8,128)(2,1)S(1)}, bf16[768,16]{0,1:T(8,128)(2,1)S(1)}, u32[]{:S(2)}, u32[]{:S(2)}) collective-permute-start(bf16[768,16]{0,1:T(8,128)(2,1)S(1)} %get-tuple-element.9), channel_id=1, source_target_pairs={{0,48},{16,64},{32,80},{48,96},{64,112},{80,128},{96,144},{112,160... | collective-permute-start | bytes 73736
  307.8 20.1 %collective-permute-start.11 = (bf16[768,16]{0,1:T(8,128)(2,1)S(1)}, bf16[768,16]{0,1:T(8,128)(2,1)S(1)}, u32[]{:S(2)}, u32[]{:S(2)}) collective-permute-start(bf16[768,16]{0,1:T(8,128)(2,1)S(1)} %get-tuple-element.9), channel_id=1, source_target_pairs={{0,64},{16,80},{32,96},{48,112},{64,128},{80,144},{96,160},{112,17... | collective-permute-start | bytes 73736
  309.1 20.7 %collective-permute-start.12 = (bf16[768,16]{0,1:T(8,128)(2,1)S(1)}, bf16[768,16]{0,1:T(8,128)(2,1)S(1)}, u32[]{:S(2)}, u32[]{:S(2)}) collective-permute-start(bf16[768,16]{0,1:T(8,128)(2,1)S(1)} %get-tuple-element.9), channel_id=1, source_target_pairs={{0,80},{16,96},{32,112},{48,128},{64,144},{80,160},{96,176},{112,1... | collective-permute-start | bytes 73736
  310.4 23.7 %collective-permute-start.13 = (bf16[768,16]{0,1:T(8,128)(2,1)S(1)}, bf16[768,16]{0,1:T(8,128)(2,1)S(1)}, u32[]{:S(2)}, u32[]{:S(2)}) collective-permute-start(bf16[768,16]{0,1:T(8,128)(2,1)S(1)} %get-tuple-element.9), channel_id=1, source_target_pairs={{0,96},{16,112},{32,128},{48,144},{64,160},{80,176},{96,192},{112,... | collective-permute-start | bytes 73736
  315.0 22.6 %collective-permute-start.14 = (bf16[768,16]{0,1:T(8,128)(2,1)S(1)}, bf16[768,16]{0,1:T(8,128)(2,1)S(1)}, u32[]{:S(2)}, u32[]{:S(2)}) collective-permute-start(bf16[768,16]{0,1:T(8,128)(2,1)S(1)} %get-tuple-element.9), channel_id=1, source_target_pairs={{0,112},{16,128},{32,144},{48,160},{64,176},{80,192},{96,208},{112... | collective-permute-start | bytes 73736
  323.6 21.1 %collective-permute-start.8 = (bf16[768,16]{0,1:T(8,128)(2,1)S(1)}, bf16[768,16]{0,1:T(8,128)(2,1)S(1)}, u32[]{:S(2)}, u32[]{:S(2)}) collective-permute-start(bf16[768,16]{0,1:T(8,128)(2,1)S(1)} %get-tuple-element.9), channel_id=1, source_target_pairs={{0,16},{16,32},{32,48},{48,64},{64,80},{80,96},{96,112},{112,128},... | collective-permute-start | bytes 73736
  328.0 21.6 %collective-permute-start.9 = (bf16[768,16]{0,1:T(8,128)(2,1)S(1)}, bf16[768,16]{0,1:T(8,128)(2,1)S(1)}, u32[]{:S(2)}, u32[]{:S(2)}) collective-permute-start(bf16[768,16]{0,1:T(8,128)(2,1)S(1)} %get-tuple-element.9), channel_id=1, source_target_pairs={{0,32},{16,48},{32,64},{48,80},{64,96},{80,112},{96,128},{112,144}... | collective-permute-start | bytes 73736
  329.9 32.2 %collective-permute-start = (bf16[768,16]{0,1:T(8,128)(2,1)S(1)}, bf16[768,16]{0,1:T(8,128)(2,1)S(1)}, u32[]{:S(2)}, u32[]{:S(2)}) collective-permute-start(bf16[768,16]{0,1:T(8,128)(2,1)S(1)} %get-tuple-element.8), channel_id=1, source_target_pairs={{0,16},{16,32},{32,48},{48,64},{64,80},{80,96},{96,112},{112,128},... | collective-permute-start | bytes 73736
  334.2 31.0 %collective-permute-start.1 = (bf16[768,16]{0,1:T(8,128)(2,1)S(1)}, bf16[768,16]{0,1:T(8,128)(2,1)S(1)}, u32[]{:S(2)}, u32[]{:S(2)}) collective-permute-start(bf16[768,16]{0,1:T(8,128)(2,1)S(1)} %get-tuple-element.8), channel_id=1, source_target_pairs={{0,32},{16,48},{32,64},{48,80},{64,96},{80,112},{96,128},{112,144}... | collective-permute-start | bytes 73736
  337.6 17.5 %collective-permute-start.7 = (bf16[768,12]{0,1:T(8,128)(2,1)S(1)}, bf16[768,12]{0,1:T(8,128)(2,1)S(1)}, u32[]{:S(2)}, u32[]{:S(2)}) collective-permute-start(bf16[768,12]{0,1:T(8,128)(2,1)S(1)} %slice.4), channel_id=1, source_target_pairs={{0,128},{16,144},{32,160},{48,176},{64,192},{80,208},{96,224},{112... | collective-permute-start | bytes 55304
  339.1 162.6 %copy-start.3 = (bf16[128,768]{1,0:T(8,128)(2,1)}, bf16[128,768]{1,0:T(8,128)(2,1)S(1)}, u32[]{:S(2)}) copy-start(bf16[128,768]{1,0:T(8,128)(2,1)S(1)} %fusion.8) | copy-start | bytes 589828
  340.8 159.7 %all-to-all-start.2 = ((bf16[32,4,768]{2,1,0:T(4,128)(2,1)}), bf16[32,4,768]{2,1,0:T(4,128)(2,1)S(1)}, u32[]{:S(2)}, u32[]{:S(2)}) async-start(bf16[32,4,768]{2,1,0:T(4,128)(2,1)} %reshape.128), calls=%async_computation.2 | async-start | bytes 393216 | tf_op jit(solution)/shard_map/all_to_all | solution.py:97
  344.6 94.3 %reduce-scatter.13.cloned.1.call-start = ((), (), s32[]{:S(2)}) async-start(), calls=%async_computation.10 | async-start | bytes 208896
  344.7 24.3 %collective-permute-start.2 = (bf16[768,16]{0,1:T(8,128)(2,1)S(1)}, bf16[768,16]{0,1:T(8,128)(2,1)S(1)}, u32[]{:S(2)}, u32[]{:S(2)}) collective-permute-start(bf16[768,16]{0,1:T(8,128)(2,1)S(1)} %get-tuple-element.8), channel_id=1, source_target_pairs={{0,48},{16,64},{32,80},{48,96},{64,112},{80,128},{96,144},{112,160... | collective-permute-start | bytes 73736
  349.5 19.5 %collective-permute-start.3 = (bf16[768,16]{0,1:T(8,128)(2,1)S(1)}, bf16[768,16]{0,1:T(8,128)(2,1)S(1)}, u32[]{:S(2)}, u32[]{:S(2)}) collective-permute-start(bf16[768,16]{0,1:T(8,128)(2,1)S(1)} %get-tuple-element.8), channel_id=1, source_target_pairs={{0,64},{16,80},{32,96},{48,112},{64,128},{80,144},{96,160},{112,17... | collective-permute-start | bytes 73736
  355.0 14.0 %collective-permute-start.4 = (bf16[768,16]{0,1:T(8,128)(2,1)S(1)}, bf16[768,16]{0,1:T(8,128)(2,1)S(1)}, u32[]{:S(2)}, u32[]{:S(2)}) collective-permute-start(bf16[768,16]{0,1:T(8,128)(2,1)S(1)} %get-tuple-element.8), channel_id=1, source_target_pairs={{0,80},{16,96},{32,112},{48,128},{64,144},{80,160},{96,176},{112,1... | collective-permute-start | bytes 73736
  362.1 7.0 %collective-permute-start.5 = (bf16[768,16]{0,1:T(8,128)(2,1)S(1)}, bf16[768,16]{0,1:T(8,128)(2,1)S(1)}, u32[]{:S(2)}, u32[]{:S(2)}) collective-permute-start(bf16[768,16]{0,1:T(8,128)(2,1)S(1)} %get-tuple-element.8), channel_id=1, source_target_pairs={{0,96},{16,112},{32,128},{48,144},{64,160},{80,176},{96,192},{112,... | collective-permute-start | bytes 73736
  365.2 3.8 collective-permute-start.6
  369.0 130.1 %reduce-scatter.11.cloned.1.call-start = ((), (), s32[]{:S(2)}) async-start(), calls=%async_computation.9 | async-start | bytes 208896
  501.7 0.7 copy-start.1
Sparse Core Ops, SparseCore 0:
  51.0 42.8 all-gather.6
  96.6 40.5 all-gather.4
  139.3 40.5 all-gather.8
  182.4 40.5 all-gather.10
  369.1 69.7 reduce-scatter.12
  441.8 57.2 reduce-scatter.10
where the time goes:
time: 511 us; the launch traced here: 509 us
  waiting for transfers between devices  251 us (49%)
  blocking collectives  124 us (24%)
  starting transfers between devices  61.5 us (12%)
  local copies, waits for them, and re-layouts  29.1 us (6%)
  matrix products  20.7 us (4%)
  between operations  15.4 us (3%)
  other arithmetic  7.92 us (2%)
    unnamed x24, waiting for transfers between devices  127 us
    unnamed x1, blocking collectives  71.2 us
    unnamed x18, starting transfers between devices  53.6 us
    all_gather x1, waiting for transfers between devices, on_device(): back_in = lax.all_gather(back_attended, 'batch', axis=0, tiled=True)  37 us
    all_gather x1, waiting for transfers between devices, on_device(): lax.all_gather(value_proj, 'batch', axis=0, tiled=True)  36.4 us
    all_gather x1, waiting for transfers between devices, on_device(): lax.all_gather(key_proj, 'batch', axis=0, tiled=True)  32.2 us
    all_to_all x1, blocking collectives, on_device(): lax.all_to_all(requests, 'storage', split_axis=0, concat_axis=0, tiled=True)  22.1 us
    all_gather x1, blocking collectives, on_device(): sum_in = lax.all_gather(row_sum.T, 'batch', axis=0, tiled=True)  15.7 us
  transfers between devices with their start and end apart: 24, of which 7 were waited for; matrix products, arithmetic and copies ran while one was open for 7% of the time, Pallas kernels for 0%

commit v1 on v0

v1 whole, which is shorter than its diff:
```python
import functools

import jax
import jax.numpy as jnp
from jax import lax
from jax.experimental import pallas as pl
from jax.experimental.pallas import tpu as pltpu
from jax.sharding import PartitionSpec as P

F32, BF16, I32 = jnp.float32, jnp.bfloat16, jnp.int32
MESH = pl.DeviceIdType.MESH
STORE = 32
RING = 8
HEADS_CORE = 3
NEG = 1e30


def iota(shape, dim):
    return lax.broadcasted_iota(I32, shape, dim)


def onehot(cond):
    return jnp.where(cond, 1.0, 0.0).astype(BF16)


def mm(a, b):
    return lax.dot_general(a, b, (((1,), (0,)), ((), ())), preferred_element_type=F32)


def mm_nt(a, b):
    return lax.dot_general(a, b, (((1,), (1,)), ((), ())), preferred_element_type=F32)


def mm_tn(a, b):
    return lax.dot_general(a, b, (((0,), (0,)), ((), ())), preferred_element_type=F32)


def kernel(
    nf_ref, hist_ref, req_ref, nbr_ref, pat_ref, owner_ref, slot_ref,
    cot_hbm, wq_hbm, wk_hbm, wv_hbm, wg_hbm, wo_hbm,
    out_ref, newh_ref, grad_ref,
    wq, wk, wv, wg, wo, wvt, wgt, cot,
    req_src, asked, found, table,
    cl_ref, cr_ref, psel, nsel, bias_ref,
    hid, qm, vt, s_ref, p_ref, acc_ref, mx_ref, gate_t, bg_t,
    gated, gsib, psend, parr, gsend, grecv, tsend, tfin,
    load_sem, cot_sems, req_sems, pull_sems, ring_send, ring_recv, sib_send, sib_recv,
    gated_sems, push_sems, gy_send, gy_recv, gf_sems,
):
    s = lax.axis_index("storage")
    b = lax.axis_index("batch")
    y = lax.div(b, 2)
    c = lax.rem(b, 2)
    sib = b + 1 - 2 * c
    win = pl.multiple_of(c * 128, 128)

    loads = [
        pltpu.make_async_copy(src.at[:, pl.ds(win, 256)], dst, load_sem.at[i])
        for i, (src, dst) in enumerate(((wq_hbm, wq), (wk_hbm, wk), (wv_hbm, wv), (wg_hbm, wg)))
    ]
    loads.append(pltpu.make_async_copy(wo_hbm, wo, load_sem.at[4]))
    loads.append(
        pltpu.make_async_copy(cot_hbm, cot.at[pl.ds(pl.multiple_of(c * 128, 128), 128)], load_sem.at[5])
    )
    for copy in loads:
        copy.start()

    barrier = pltpu.get_barrier_semaphore()

    def greet_store(k, _):
        peer = lax.rem(s + k, STORE)
        pl.semaphore_signal(barrier, inc=1, device_id=(peer, b), device_id_type=MESH)
        pl.semaphore_signal(barrier, inc=1, device_id=(peer, sib), device_id_type=MESH)
        return 0

    lax.fori_loop(1, STORE, greet_store, 0)
    pl.semaphore_signal(barrier, inc=1, device_id=(s, sib), device_id_type=MESH)

    def greet_ring(k, _):
        peer = lax.rem(y + k, RING) * 2 + c
        pl.semaphore_signal(barrier, inc=1, device_id=(s, peer), device_id_type=MESH)
        return 0

    lax.fori_loop(1, RING, greet_ring, 0)

    req_src[...] = jnp.zeros_like(req_src)
    req_src[:, 0, 0:8] = req_ref[...]
    pl.semaphore_wait(barrier, 2 * (STORE - 1) + 1 + RING - 1)

    def store_copy(src, dst, sems, peer):
        return pltpu.make_async_remote_copy(
            src_ref=src, dst_ref=dst, send_sem=sems.at[0], recv_sem=sems.at[1],
            device_id=(peer, b), device_id_type=MESH,
        )

    def send_all(src, dst, sems):
        def body(k, _):
            peer = lax.rem(s + k, STORE)
            store_copy(src.at[peer], dst.at[s], sems, peer).start()
            return 0

        lax.fori_loop(1, STORE, body, 0)

    def bulk_wait(ref, sem):
        pltpu.make_async_copy(ref, ref, sem).wait()

    others = pl.ds(0, STORE - 1)

    send_all(req_src, asked, req_sems)
    asked[s] = req_src[s]
    cot_copy = pltpu.make_async_remote_copy(
        src_ref=cot_hbm, dst_ref=cot.at[pl.ds(pl.multiple_of(c * 128, 128), 128)],
        send_sem=cot_sems.at[0], recv_sem=cot_sems.at[1],
        device_id=(s, sib), device_id_type=MESH,
    )
    cot_copy.start()

    hist_b = hist_ref[...].astype(BF16)
    rep = onehot(iota((STORE * 16, STORE), 1) == (iota((STORE * 16, STORE), 0) >> 4))
    bulk_wait(asked.at[others], req_sems.at[1])

    asked_f = asked[...].reshape(STORE, 128).astype(F32).astype(BF16)
    spread = mm(rep, asked_f)
    prow = iota((STORE * 16, 128), 0)
    lane = iota((STORE * 16, 128), 1)
    mine = jnp.sum(jnp.where(lane == (prow & 7), spread, 0.0), axis=1, keepdims=True).astype(I32)
    hit = mine == lane
    pick_l = onehot(hit & ((prow & 8) == 0))
    pick_r = onehot(hit & ((prow & 8) != 0))
    rows = mm(pick_l, hist_b[:, :384]) + mm(pick_r, hist_b[:, 384:])
    found[...] = rows.astype(BF16).reshape(STORE, 16, 384)
    send_all(found, table, pull_sems)
    table[s] = found[s]

    nbr = nbr_ref[...]
    at = iota((128, 256), 1)
    count = jnp.zeros((128, 256), F32)
    for k in range(16):
        count = count + jnp.where(nbr[:, k : k + 1] == at, 1.0, 0.0)
    count = count.astype(BF16)
    src_i = iota((256, 512), 0)
    dst_i = iota((256, 512), 1)
    home = src_i + (src_i & -8)
    cl_ref[...] = mm(count, onehot(dst_i == home)).astype(BF16)
    cr_ref[...] = mm(count, onehot(dst_i == home + 8)).astype(BF16)

    owner_row = owner_ref[...]
    i0 = iota((128, 128), 0)
    i1 = iota((128, 128), 1)
    owner_all = jnp.broadcast_to(owner_row, (128, 128))
    owner_col = jnp.sum(jnp.where(i0 == i1, owner_all, 0), axis=1, keepdims=True)
    rank = jnp.sum(
        jnp.where((owner_col == owner_all) & (i0 < i1), 1, 0), axis=0, keepdims=True
    )
    pos = owner_row * 4 + rank
    pr = iota((512, 128), 0)
    place = ((pr >> 4) << 2) + (pr & 3) == pos
    for u in range(3):
        psel[u] = onehot(place & (((pr >> 2) & 3) == u))
    slots = slot_ref[...]
    kk = iota((STORE, 512), 1)
    flat = jnp.zeros((STORE, 512), I32)
    for e in range(4):
        flat = flat + jnp.where((kk & 3) == e, slots[:, e : e + 1], 0)
    slot_row = jnp.sum(
        jnp.where((kk >> 4) == iota((STORE, 512), 0), flat, 0), axis=0, keepdims=True
    )
    kc = iota((128, 512), 1)
    lands = iota((128, 512), 0) == slot_row
    for u in range(3):
        nsel[u] = onehot(lands & (((kc >> 2) & 3) == u))

    qsel = onehot(iota((16, 256), 0) == 2 * y + (iota((16, 256), 1) >> 7))
    seen = mm_tn(pat_ref[...].astype(F32).astype(BF16), qsel)
    bias_ref[...] = (seen - 1.0) * NEG
    mx_ref[...] = jnp.full_like(mx_ref, -2.0 * NEG)

    for copy in loads:
        copy.wait()
    wvt[...] = wv[...].T
    wgt[...] = wg[...].T

    bulk_wait(table.at[others], pull_sems.at[1])
    t2 = table[...].reshape(STORE * 16, 384)
    my_rows = pl.multiple_of(b * 128, 128)
    hid[pl.ds(my_rows, 128), 0:384] = (
        nf_ref[:, 0:384].astype(F32) + mm(cl_ref[...], t2) * (1.0 / 16)
    ).astype(BF16)
    hid[pl.ds(my_rows, 128), 384:768] = (
        nf_ref[:, 384:768].astype(F32) + mm(cr_ref[...], t2) * (1.0 / 16)
    ).astype(BF16)

    right = lax.rem(y + 1, RING)
    left = lax.rem(y + RING - 1, RING)

    def chip_at(direction, dist):
        return lax.rem(y + (RING - dist if direction == 0 else dist), RING)

    def half_of(chip, core, half):
        return hid.at[pl.ds(pl.multiple_of(chip * 256 + core * 128 + half * 64, 64), 64)]

    def ring_copy(direction, dist, half, chip):
        ref = half_of(chip, c, half)
        idx = (direction * 4 + dist - 1) * 2 + half
        to = right if direction == 0 else left
        return pltpu.make_async_remote_copy(
            src_ref=ref, dst_ref=ref, send_sem=ring_send.at[idx], recv_sem=ring_recv.at[idx],
            device_id=(s, to * 2 + c), device_id_type=MESH,
        )

    def sib_copy(direction, dist, half, chip, core):
        ref = half_of(chip, core, half)
        idx = (direction * 4 + (dist if dist else 0) - 1) * 2 + half if dist else 16 + half
        return pltpu.make_async_remote_copy(
            src_ref=ref, dst_ref=ref, send_sem=sib_send.at[idx], recv_sem=sib_recv.at[idx],
            device_id=(s, sib), device_id_type=MESH,
        )

    def halves(direction, dist):
        if dist < 4:
            return (0, 1)
        return (0,) if direction == 0 else (1,)

    sent = []

    def go(copy):
        copy.start()
        sent.append(copy)

    for half in (0, 1):
        for direction in (0, 1):
            go(ring_copy(direction, 1, half, y))
        go(sib_copy(0, 0, half, y, c))

    def wait_sib(direction, dist):
        chip = chip_at(direction, dist)
        for half in halves(direction, dist) if dist else (0, 1):
            sib_copy(direction, dist, half, chip, 1 - c).wait_recv()

    def process(chip):
        r0 = pl.multiple_of(chip * 256, 256)
        hc = hid[pl.ds(r0, 256), :]
        kc_ = mm(hc, wk[...]).astype(BF16)
        vt[chip] = mm_nt(wvt[...], hc).astype(BF16)
        b0 = bias_ref[pl.ds(2 * chip, 1), :]
        b1 = bias_ref[pl.ds(2 * chip + 1, 1), :]
        for h in range(HEADS_CORE):
            sc = mm_nt(kc_, qm[h])
            lo = sc[0:128] + b0
            hi = sc[128:256] + b1
            s_ref[h, pl.ds(r0, 128), :] = lo
            s_ref[h, pl.ds(r0 + 128, 128), :] = hi
            top = jnp.max(jnp.maximum(lo, hi), axis=0, keepdims=True)
            mx_ref[h : h + 1, :] = jnp.maximum(mx_ref[h : h + 1, :], top)

    dcol = iota((256, 256), 0) - c * 64
    masks = [(dcol >> 6) == h for h in range(HEADS_CORE)]
    my_chip = pl.multiple_of(y * 256, 256)

    for dist in range(1, 5):
        for half in (0, 1):
            for direction in (0, 1):
                if half not in halves(direction, dist):
                    continue
                chip = chip_at(direction, dist)
                ring_copy(direction, dist, half, chip).wait_recv()
                if dist < 4 and half in halves(direction, dist + 1):
                    go(ring_copy(direction, dist + 1, half, chip))
                go(sib_copy(direction, dist, half, chip, c))
        if dist == 1:
            wait_sib(0, 0)
            hc = hid[pl.ds(my_chip, 256), :]
            q = (mm(hc, wq[...]) * 0.125).astype(BF16).astype(F32)
            lq = (iota((256, 256), 1) - c * 64) >> 6
            for h in range(HEADS_CORE):
                qm[h] = jnp.where(lq == h, q, 0.0).astype(BF16)
            gate_t[...] = mm_nt(wgt[...], hc).astype(BF16)
            cot_copy.wait_recv()
            bg_t[...] = mm_nt(wo[pl.ds(win, 256), :], cot[...]).astype(BF16)
            process(y)
        else:
            for direction in (0, 1):
                wait_sib(direction, dist - 1)
                process(chip_at(direction, dist - 1))
    wait_sib(0, 4)
    wait_sib(1, 4)
    process(chip_at(0, 4))

    acc_ref[...] = jnp.zeros_like(acc_ref)

    def soft(j, sums):
        r0 = pl.multiple_of(j * 256, 256)
        new = []
        for h in range(HEADS_CORE):
            p = jnp.exp(s_ref[h, pl.ds(r0, 256), :] - mx_ref[h : h + 1, :])
            new.append(sums[h] + jnp.sum(p, axis=0, keepdims=True))
            pb = p.astype(BF16)
            p_ref[h, pl.ds(r0, 256), :] = pb
            acc_ref[h] += mm(vt[j], pb)
        return tuple(new)

    zero_row = jnp.zeros((1, 256), F32)
    sums = lax.fori_loop(0, RING, soft, (zero_row,) * HEADS_CORE)
    inv = jnp.zeros((256, 256), F32)
    att = jnp.zeros((256, 256), F32)
    for h in range(HEADS_CORE):
        one = 1.0 / sums[h]
        inv = jnp.where(masks[h], one, inv)
        att = jnp.where(masks[h], acc_ref[h] * one, att)
    att = att.astype(BF16).astype(F32)
    gate = gate_t[...].astype(F32)
    bg = bg_t[...].astype(F32)
    gated_t = (att * gate).astype(BF16)
    for qb in (0, 1):
        gated[qb] = gated_t[:, qb * 128 : (qb + 1) * 128]
    gated_copy = pltpu.make_async_remote_copy(
        src_ref=gated.at[1 - c], dst_ref=gsib, send_sem=gated_sems.at[0],
        recv_sem=gated_sems.at[1], device_id=(s, sib), device_id_type=MESH,
    )
    gated_copy.start()

    def send_grad(which, grad_t):
        gsend[which] = grad_t.T.astype(BF16)
        my_part = pl.multiple_of(y * 96, 32)
        grecv[which, y] = gsend[which, pl.ds(my_part, 96), :]

        def body(k, _):
            to = lax.rem(y + k, RING)
            pltpu.make_async_remote_copy(
                src_ref=gsend.at[which, pl.ds(pl.multiple_of(to * 96, 32), 96)],
                dst_ref=grecv.at[which, y],
                send_sem=gy_send.at[which], recv_sem=gy_recv.at[which],
                device_id=(s, to * 2 + c), device_id_type=MESH,
            ).start()
            return 0

        lax.fori_loop(1, RING, body, 0)

    send_grad(0, mm((bg * att).astype(BF16), hid[pl.ds(my_chip, 256), :]))

    gated_copy.wait_recv()
    out = nf_ref[...].astype(F32) + (
        mm_tn(gated[c], wo[pl.ds(win, 256), :])
        + mm_tn(gsib[...], wo[pl.ds(pl.multiple_of((1 - c) * 128, 128), 256), :])
    )
    out_b = out.astype(BF16)
    out_ref[...] = out_b
    pushed = mm(psel[0], out_b[:, 0:256])
    pushed = pushed + mm(psel[1], out_b[:, 256:512])
    pushed = pushed + mm(psel[2], out_b[:, 512:768])
    psend[...] = pushed.astype(BF16).reshape(STORE, 16, 256)
    send_all(psend, parr, push_sems)
    parr[s] = psend[s]

    back = (bg * gate).astype(BF16).astype(F32) * inv
    backs = [jnp.where(masks[h], back, 0.0).astype(BF16) for h in range(HEADS_CORE)]

    def value_part(j, total):
        r0 = pl.multiple_of(j * 256, 256)
        dv = mm_nt(backs[0], p_ref[0, pl.ds(r0, 256), :])
        dv = dv + mm_nt(backs[1], p_ref[1, pl.ds(r0, 256), :])
        dv = dv + mm_nt(backs[2], p_ref[2, pl.ds(r0, 256), :])
        return total + mm(dv.astype(BF16), hid[pl.ds(r0, 256), :])

    send_grad(1, lax.fori_loop(0, RING, value_part, jnp.zeros((256, 768), F32)))

    bulk_wait(parr.at[others], push_sems.at[1])
    arrived = parr[...].reshape(STORE * 16, 256)
    for u in range(3):
        newh_ref[:, u * 256 : (u + 1) * 256] = mm(nsel[u], arrived).astype(BF16)

    rr = iota((96, 256), 0)
    ll = iota((96, 256), 1)
    lm = ll & 127
    row_of = rr - (ll >> 7) * 48
    spread_g = onehot((row_of == lm) & (lm < 48))
    spread_v = onehot((row_of == lm - 64) & (lm >= 64) & (lm < 112))
    e0 = iota((256, 256), 0)
    e1 = iota((256, 256), 1)
    col_pick = onehot((e1 == c * 64 + (e0 >> 4) * 12 + (e0 & 15)) & ((e0 & 15) < 12))
    sums_y = []
    for which in (0, 1):
        bulk_wait(grecv.at[which, pl.ds(0, RING - 1)], gy_recv.at[which])
        total = grecv[which, 0].astype(F32)
        for j in range(1, RING):
            total = total + grecv[which, j].astype(F32)
        sums_y.append(total.astype(BF16))
    mixed = mm_tn(sums_y[0], spread_g) + mm_tn(sums_y[1], spread_v)
    tiles = mm(col_pick, mixed.astype(BF16)).astype(BF16)
    for core in (0, 1):
        tsend[core] = tiles[:, core * 128 : (core + 1) * 128].reshape(16, 16, 128)
    in_half = lax.div(s, 16)

    def send_tile(i, _):
        dest = lax.div(i, 2)
        core = lax.rem(i, 2)
        to = c * 16 + dest
        own = (to == s) & (core == c)

        @pl.when(own)
        def _():
            tfin[s] = tsend[core, dest]

        @pl.when(jnp.logical_not(own))
        def _():
            pltpu.make_async_remote_copy(
                src_ref=tsend.at[core, dest], dst_ref=tfin.at[s],
                send_sem=gf_sems.at[0], recv_sem=gf_sems.at[1],
                device_id=(to, y * 2 + core), device_id_type=MESH,
            ).start()

        return 0

    lax.fori_loop(0, 32, send_tile, 0)

    @pl.when(in_half == c)
    def _():
        bulk_wait(tfin.at[others], gf_sems.at[1])
        bulk_wait(tfin.at[others], gf_sems.at[0])

    @pl.when(in_half != c)
    def _():
        bulk_wait(tfin, gf_sems.at[1])
        bulk_wait(tfin, gf_sems.at[0])

    final = tfin[0].astype(F32)
    for j in range(1, STORE):
        final = final + tfin[j].astype(F32)
    grad_ref[...] = final

    bulk_wait(req_src.at[others], req_sems.at[0])
    bulk_wait(found.at[others], pull_sems.at[0])
    bulk_wait(psend.at[others], push_sems.at[0])
    cot_copy.wait_send()
    for copy in sent:
        copy.wait_send()
    gated_copy.wait_send()
    for which in (0, 1):
        bulk_wait(grecv.at[which, pl.ds(0, RING - 1)], gy_send.at[which])


def on_device(
    node_features, history, requests, neighbours, pattern, push_owner, push_slot,
    w_query, w_key, w_value, w_gate, w_out, cotangent,
):
    vmem = pl.BlockSpec(memory_space=pltpu.VMEM)
    hbm = pl.BlockSpec(memory_space=pl.ANY)
    out, newh, grads = pl.pallas_call(
        kernel,
        out_shape=(
            jax.ShapeDtypeStruct((128, 768), BF16),
            jax.ShapeDtypeStruct((128, 768), BF16),
            jax.ShapeDtypeStruct((16, 128), F32),
        ),
        in_specs=[vmem] * 7 + [hbm] * 6,
        out_specs=(vmem, vmem, vmem),
        scratch_shapes=[
            pltpu.VMEM((768, 256), BF16),
            pltpu.VMEM((768, 256), BF16),
            pltpu.VMEM((768, 256), BF16),
            pltpu.VMEM((768, 256), BF16),
            pltpu.VMEM((384, 768), BF16),
            pltpu.VMEM((256, 768), BF16),
            pltpu.VMEM((256, 768), BF16),
            pltpu.VMEM((256, 768), BF16),
            pltpu.VMEM((STORE, 1, 128), I32),
            pltpu.VMEM((STORE, 1, 128), I32),
            pltpu.VMEM((STORE, 16, 384), BF16),
            pltpu.VMEM((STORE, 16, 384), BF16),
            pltpu.VMEM((128, 512), BF16),
            pltpu.VMEM((128, 512), BF16),
            pltpu.VMEM((3, 512, 128), BF16),
            pltpu.VMEM((3, 128, 512), BF16),
            pltpu.VMEM((16, 256), F32),
            pltpu.VMEM((2048, 768), BF16),
            pltpu.VMEM((3, 256, 256), BF16),
            pltpu.VMEM((8, 256, 256), BF16),
            pltpu.VMEM((3, 2048, 256), F32),
            pltpu.VMEM((3, 2048, 256), BF16),
            pltpu.VMEM((3, 256, 256), F32),
            pltpu.VMEM((8, 256), F32),
            pltpu.VMEM((256, 256), BF16),
            pltpu.VMEM((256, 256), BF16),
            pltpu.VMEM((2, 256, 128), BF16),
            pltpu.VMEM((256, 128), BF16),
            pltpu.VMEM((STORE, 16, 256), BF16),
            pltpu.VMEM((STORE, 16, 256), BF16),
            pltpu.VMEM((2, 768, 256), BF16),
            pltpu.VMEM((2, 8, 96, 256), BF16),
            pltpu.VMEM((2, 16, 16, 128), BF16),
            pltpu.VMEM((STORE, 16, 128), BF16),
            pltpu.SemaphoreType.DMA((6,)),
            pltpu.SemaphoreType.DMA((2,)),
            pltpu.SemaphoreType.DMA((2,)),
            pltpu.SemaphoreType.DMA((2,)),
            pltpu.SemaphoreType.DMA((16,)),
            pltpu.SemaphoreType.DMA((16,)),
            pltpu.SemaphoreType.DMA((18,)),
            pltpu.SemaphoreType.DMA((18,)),
            pltpu.SemaphoreType.DMA((2,)),
            pltpu.SemaphoreType.DMA((2,)),
            pltpu.SemaphoreType.DMA((2,)),
            pltpu.SemaphoreType.DMA((2,)),
            pltpu.SemaphoreType.DMA((2,)),
        ],
        compiler_params=pltpu.CompilerParams(
            collective_id=0, has_side_effects=True, vmem_limit_bytes=48 * 1024 * 1024
        ),
        cost_estimate=pl.CostEstimate(
            flops=7_000_000_000, bytes_accessed=6_000_000, transcendentals=1_600_000
        ),
    )(
        node_features, history, requests, neighbours, pattern, push_owner.reshape(1, -1), push_slot,
        cotangent, w_query, w_key, w_value, w_gate, w_out,
    )
    return (
        out,
        newh.astype(F32),
        grads[0:12, 0:48].T,
        grads[0:12, 64:112].T,
    )


def solution(mesh):
    rows = P(("storage", "batch"), None)
    in_specs = (
        rows, rows, rows, rows, P("storage", None), P(("storage", "batch")), rows,
        P(), P(), P(), P(), P(), rows,
    )
    out_specs = (rows, rows, P("batch", "storage"), P("batch", "storage"))
    return jax.shard_map(
        on_device, mesh=mesh, in_specs=in_specs, out_specs=out_specs, check_vma=False
    )
```

time: 511 us -> 101 us (0.20)
  waiting for transfers between devices: 251 us -> 0 us
  blocking collectives: 124 us -> 0 us
  Pallas kernels: 0 us -> 87.8 us
  starting transfers between devices: 61.5 us -> 0 us
  matrix products: 20.7 us -> 0 us
  local copies, waits for them, and re-layouts: 29.1 us -> 11.7 us
  between operations: 15.4 us -> 0.66 us
  other arithmetic: 7.92 us -> 0.77 us
    unnamed x24 -> x0, waiting for transfers between devices: 127 us -> none
    all_gather x4 -> x0, waiting for transfers between devices: 115 us -> none  [the longest x1 37 us: on_device(): back_in = lax.all_gather(back_attended, 'batch', axis=0, tiled=True)]
    pallas_call x0 -> x1, Pallas kernels: none -> 87.8 us  [on_device(): pl.pallas_call(kernel, out_shape=(jax.ShapeDtypeStruct((128, 768), BF16),...]
    unnamed x1 -> x0, blocking collectives: 71.2 us -> none
    unnamed x18 -> x0, starting transfers between devices: 53.6 us -> none
    all_gather x2 -> x0, blocking collectives: 30.7 us -> none  [the longest x1 15.7 us: on_device(): sum_in = lax.all_gather(row_sum.T, 'batch', axis=0, tiled=True)]
    all_to_all x1 -> x0, blocking collectives: 22.1 us -> none  [on_device(): lax.all_to_all(requests, 'storage', split_axis=0, concat_axis=0, tiled=True)]
    dot_general x12 -> x0, matrix products: 20.7 us -> none  [the longest x1 6.84 us: on_device(): jnp.einsum('hqk,qhd->khd', weights, back_in.reshape(arriving, HEADS, HEAD...]
  transfers between devices with their start and end apart: 24 -> 0, of which waited for: 7 -> 0; matrix products, arithmetic and copies ran while one was open for 7% -> 0% of each run, Pallas kernels for 0% -> 0%
where the time goes in v1:
time: 101 us
  Pallas kernels  87.8 us (87%)
  local copies, waits for them, and re-layouts  11.7 us (12%)
    pallas_call x1, Pallas kernels, on_device(): pl.pallas_call(kernel, out_shape=(jax.ShapeDtypeStruct((128, 768), BF16),...  87.8 us
    unnamed x28, local copies, waits for them, and re-layouts  11 us

profile of v1, /device:TPU:1, one launch (start us, length us, event | category | flops | bytes accessed | tf_op | source)
XLA Modules:
  0.0 100.9 jit_solution(14786217610025601872)
XLA Ops:
  0.6 0.0 copy-start.10
  0.6 0.8 copy.17.req_ref
  1.4 0.0 copy-done.10
  1.4 0.0 copy-start.11
  1.4 0.1 copy.18.nbr_ref
  1.5 0.6 copy-done.11
  2.1 0.0 copy-start.8
  2.1 0.0 copy-start.9
  2.1 0.1 copy.19.slot_ref
  2.2 0.6 copy-done.8
  2.8 0.0 copy-done.9
  2.8 0.0 copy-start
  2.8 1.1 %copy-done = bf16[768,384]{1,0:T(8,128)(2,1)S(1)} copy-done((bf16[768,384]{1,0:T(8,128)(2,1)S(1)}, bf16[768,384]{1,0:T(8,128)(2,1)}, u32[]{:S(2)}) %copy-start) | copy-done | bytes 589848
  3.9 0.0 copy-start.1
  3.9 1.1 %copy-done.1 = bf16[768,384]{1,0:T(8,128)(2,1)S(1)} copy-done((bf16[768,384]{1,0:T(8,128)(2,1)S(1)}, bf16[768,384]{1,0:T(8,128)(2,1)}, u32[]{:S(2)}) %copy-start.1) | copy-done | bytes 589848
  4.9 0.0 copy-start.2
  4.9 1.1 %copy-done.2 = bf16[768,384]{1,0:T(8,128)(2,1)S(1)} copy-done((bf16[768,384]{1,0:T(8,128)(2,1)S(1)}, bf16[768,384]{1,0:T(8,128)(2,1)}, u32[]{:S(2)}) %copy-start.2) | copy-done | bytes 589848
  6.0 0.0 copy-start.3
  6.0 1.1 %copy-done.3 = bf16[768,384]{1,0:T(8,128)(2,1)S(1)} copy-done((bf16[768,384]{1,0:T(8,128)(2,1)S(1)}, bf16[768,384]{1,0:T(8,128)(2,1)}, u32[]{:S(2)}) %copy-start.3) | copy-done | bytes 589848
  7.1 0.0 copy-start.4
  7.1 1.1 %copy-done.4 = bf16[384,768]{1,0:T(8,128)(2,1)S(1)} copy-done((bf16[384,768]{1,0:T(8,128)(2,1)S(1)}, bf16[384,768]{1,0:T(8,128)(2,1)}, u32[]{:S(2)}) %copy-start.4) | copy-done | bytes 589848
  8.1 0.0 copy-start.5
  8.1 1.0 copy-done.5
  9.1 0.0 copy-start.6
  9.1 0.9 copy-done.6
  10.0 0.0 copy-start.7
  10.0 0.9 copy-done.7
  11.0 87.8 %shard_map.156 = (bf16[128,768]{1,0:T(8,128)(2,1)S(1)}, bf16[128,768]{1,0:T(8,128)(2,1)S(1)}, f32[16,128]{1,0:T(8,128)S(1)}) custom-call(bf16[128,768]{1,0:T(8,128)(2,1)S(1)} %copy-done.6, f32[128,768]{1,0:T(8,128)S(1)} %copy-done.5, s32[32,8]{1,0:T(8,128)S(1)} %copy.17.req_ref, s32[128,16]{1,0:T(8,128)S(1)} %copy.18.nbr_ref, s32[16,16]{1,0:T(8,128)S(1)} %copy-done.8, ...), custom_call_target="tpu_custom_call" | custom-call | flops 7000000000 | bytes 6000000 | tf_op jit(solution)/shard_map/pallas_call | solution.py:448
  98.8 0.8 convert_element_type.3
  99.6 0.7 slice_bitcast_fusion
  100.2 0.7 copy.21
Async XLA Ops:
  0.6 0.8 copy-start.10
  1.4 0.7 copy-start.11
  2.1 0.7 copy-start.8
  2.1 0.7 copy-start.9
  2.8 1.1 %copy-start = (bf16[768,384]{1,0:T(8,128)(2,1)S(1)}, bf16[768,384]{1,0:T(8,128)(2,1)}, u32[]{:S(2)}) copy-start(bf16[768,384]{1,0:T(8,128)(2,1)} %wq_hbm.1) | copy-start | bytes 1769476
  3.9 1.1 %copy-start.1 = (bf16[768,384]{1,0:T(8,128)(2,1)S(1)}, bf16[768,384]{1,0:T(8,128)(2,1)}, u32[]{:S(2)}) copy-start(bf16[768,384]{1,0:T(8,128)(2,1)} %wk_hbm.1) | copy-start | bytes 1769476
  4.9 1.1 %copy-start.2 = (bf16[768,384]{1,0:T(8,128)(2,1)S(1)}, bf16[768,384]{1,0:T(8,128)(2,1)}, u32[]{:S(2)}) copy-start(bf16[768,384]{1,0:T(8,128)(2,1)} %wv_hbm.1) | copy-start | bytes 1769476
  6.0 1.1 %copy-start.3 = (bf16[768,384]{1,0:T(8,128)(2,1)S(1)}, bf16[768,384]{1,0:T(8,128)(2,1)}, u32[]{:S(2)}) copy-start(bf16[768,384]{1,0:T(8,128)(2,1)} %wg_hbm.1) | copy-start | bytes 1769476
  7.1 1.1 %copy-start.4 = (bf16[384,768]{1,0:T(8,128)(2,1)S(1)}, bf16[384,768]{1,0:T(8,128)(2,1)}, u32[]{:S(2)}) copy-start(bf16[384,768]{1,0:T(8,128)(2,1)} %wo_hbm.1) | copy-start | bytes 1769476
  8.1 1.0 copy-start.5
  9.1 0.9 copy-start.6
  10.0 0.9 copy-start.7

commit v2 on v1

v2 whole, which is shorter than its diff:
```python
import functools

import jax
import jax.numpy as jnp
from jax import lax
from jax.experimental import pallas as pl
from jax.experimental.pallas import tpu as pltpu
from jax.sharding import PartitionSpec as P

F32, BF16, I32 = jnp.float32, jnp.bfloat16, jnp.int32
MESH = pl.DeviceIdType.MESH
STORE = 32
RING = 8
HEADS_CORE = 3
NEG = 1e30


def iota(shape, dim):
    return lax.broadcasted_iota(I32, shape, dim)


def onehot(cond):
    return jnp.where(cond, 1.0, 0.0).astype(BF16)


def mm(a, b):
    return lax.dot_general(a, b, (((1,), (0,)), ((), ())), preferred_element_type=F32)


def mm_nt(a, b):
    return lax.dot_general(a, b, (((1,), (1,)), ((), ())), preferred_element_type=F32)


def mm_tn(a, b):
    return lax.dot_general(a, b, (((0,), (0,)), ((), ())), preferred_element_type=F32)


def kernel(
    nf_hbm, hist_hbm, req_hbm, nbr_hbm, pat_hbm, owner_hbm, slot_hbm,
    cot_hbm, wq_hbm, wk_hbm, wv_hbm, wg_hbm, wo_hbm,
    out_ref, newh_ref, grad_ref,
    nf_ref, hist_ref, req_ref, nbr_ref, pat_ref, owner_ref, slot_ref,
    wq, wk, wv, wg, wo, wvt, wgt, cot,
    req_src, asked, found, table, mix, psel, nsel, bias_ref, lanes96,
    hid, qm, p_ref, acc_ref, mx_ref, sum_ref, mx_chip, gate_t, bg_t,
    gated, gsib, psend, parr, vsend, vrecv, tsend, tfin, gsend, grecv, hsend, gfin,
    load_sem, small_sem, cot_sems, req_sems, pull_send, pull_recv,
    ring_send, ring_recv, sib_send, sib_recv,
    gated_sems, push_sems, vy_sems, vs_sems, gs_sems, gy_sems,
):
    s = lax.axis_index("storage")
    b = lax.axis_index("batch")
    y = lax.div(b, 2)
    c = lax.rem(b, 2)
    sib = b + 1 - 2 * c
    in_half = lax.div(s, 16)
    win = pl.multiple_of(c * 128, 128)
    c64 = pl.multiple_of(c * 64, 64)

    small = [
        pltpu.make_async_copy(src, dst, small_sem.at[i])
        for i, (src, dst) in enumerate((
            (req_hbm, req_ref), (hist_hbm, hist_ref), (nbr_hbm, nbr_ref), (owner_hbm, owner_ref),
            (slot_hbm, slot_ref), (pat_hbm, pat_ref), (nf_hbm, nf_ref),
        ))
    ]
    for copy in small:
        copy.start()
    loads = [
        pltpu.make_async_copy(src.at[:, pl.ds(win, 256)], dst, load_sem.at[i])
        for i, (src, dst) in enumerate(((wq_hbm, wq), (wk_hbm, wk), (wv_hbm, wv), (wg_hbm, wg)))
    ]
    loads.append(pltpu.make_async_copy(wo_hbm, wo, load_sem.at[4]))
    loads.append(pltpu.make_async_copy(cot_hbm, cot.at[pl.ds(win, 128)], load_sem.at[5]))
    for copy in loads:
        copy.start()

    barrier = pltpu.get_barrier_semaphore()

    def greet_store(k, _):
        peer = lax.rem(s + k, STORE)
        pl.semaphore_signal(barrier, inc=1, device_id=(peer, b), device_id_type=MESH)
        pl.semaphore_signal(barrier, inc=1, device_id=(peer, sib), device_id_type=MESH)
        return 0

    lax.fori_loop(1, STORE, greet_store, 0)

    def greet_ring(k, _):
        peer = lax.rem(b + k, 2 * RING)
        pl.semaphore_signal(barrier, inc=1, device_id=(s, peer), device_id_type=MESH)
        return 0

    lax.fori_loop(1, 2 * RING, greet_ring, 0)

    small[0].wait()
    eye8 = onehot(iota((8, 128), 0) == iota((8, 128), 1))
    req_src[...] = mm_tn(req_ref[...].astype(F32).astype(BF16), eye8).astype(I32).reshape(STORE, 1, 128)
    pl.semaphore_wait(barrier, 2 * (STORE - 1) + 2 * RING - 1)

    def store_copy(src, dst, send_sem, recv_sem, peer):
        return pltpu.make_async_remote_copy(
            src_ref=src, dst_ref=dst, send_sem=send_sem, recv_sem=recv_sem,
            device_id=(peer, b), device_id_type=MESH,
        )

    def send_all(src, dst, send_sem, recv_sem):
        def body(k, _):
            peer = lax.rem(s + k, STORE)
            store_copy(src.at[peer], dst.at[s], send_sem, recv_sem, peer).start()
            return 0

        lax.fori_loop(1, STORE, body, 0)

    def bulk_wait(ref, sem):
        pltpu.make_async_copy(ref, ref, sem).wait()

    others = pl.ds(0, STORE - 1)

    send_all(req_src, asked, req_sems.at[0], req_sems.at[1])
    asked[s] = req_src[s]
    cot_copy = pltpu.make_async_remote_copy(
        src_ref=cot_hbm, dst_ref=cot.at[pl.ds(win, 128)],
        send_sem=cot_sems.at[0], recv_sem=cot_sems.at[1],
        device_id=(s, sib), device_id_type=MESH,
    )
    cot_copy.start()

    for copy in small[1:]:
        copy.wait()
    hist_b = hist_ref[...].astype(BF16)
    hist_l = jnp.concatenate([hist_b[:, p * 256 : p * 256 + 128] for p in range(3)], axis=1)
    hist_r = jnp.concatenate([hist_b[:, p * 256 + 128 : p * 256 + 256] for p in range(3)], axis=1)
    rep = onehot(iota((STORE * 16, STORE), 1) == (iota((STORE * 16, STORE), 0) >> 4))
    nbr = nbr_ref[...]
    at = iota((256, 128), 0)
    count = jnp.zeros((256, 128), F32)
    for k in range(16):
        count = count + jnp.where(nbr[k : k + 1, :] == at, 1.0, 0.0)
    count = count.astype(BF16)
    src_i = iota((256, 512), 0)
    dst_i = iota((256, 512), 1)
    home = src_i + (src_i & -8)
    mix[0:128] = mm_tn(count, onehot(dst_i == home)).astype(BF16)
    mix[128:256] = mm_tn(count, onehot(dst_i == home + 8)).astype(BF16)

    bulk_wait(asked.at[others], req_sems.at[1])

    asked_f = asked[...].reshape(STORE, 128).astype(F32).astype(BF16)
    spread = mm(rep, asked_f)
    prow = iota((STORE * 16, 128), 0)
    lane = iota((STORE * 16, 128), 1)
    mine = jnp.sum(jnp.where(lane == (prow & 7), spread, 0.0), axis=1, keepdims=True).astype(I32)
    hit = mine == lane
    pick_l = onehot(hit & ((prow & 8) == 0))
    pick_r = onehot(hit & ((prow & 8) != 0))
    rows = (mm(pick_l, hist_l) + mm(pick_r, hist_r)).astype(BF16)
    for p in range(3):
        found[p] = rows[:, p * 128 : (p + 1) * 128].reshape(STORE, 16, 128)
    for p in range(3):
        send_all(found.at[p], table.at[p], pull_send.at[p], pull_recv.at[p])
    for p in range(3):
        table[p, s] = found[p, s]

    for copy in loads:
        copy.wait()
    wvt[...] = wv[...].T
    wgt[...] = wg[...].T
    qsel = onehot(iota((16, 256), 0) == 2 * y + (iota((16, 256), 1) >> 7))
    seen = mm_tn(pat_ref[...].astype(F32).astype(BF16), qsel)
    bias_ref[...] = (seen - 1.0) * NEG
    mx_ref[...] = jnp.full_like(mx_ref, -2.0 * NEG)
    sum_ref[...] = jnp.zeros_like(sum_ref)
    acc_ref[...] = jnp.zeros_like(acc_ref)
    cot_copy.wait_recv()
    wo_mine = pl.multiple_of(c * 192, 64)
    wo_sib = pl.multiple_of((1 - c) * 192, 64)
    bg_t[...] = mm_nt(wo[pl.ds(wo_mine, 192), :], cot[...]).astype(BF16)

    lr = iota((768, 1024), 0)
    ll = iota((768, 1024), 1)
    lanes96[...] = onehot((lr == (ll >> 7) * 96 + (ll & 127)) & ((ll & 127) < 96))

    owner_row = owner_ref[...]
    i0 = iota((128, 128), 0)
    i1 = iota((128, 128), 1)
    owner_all = jnp.broadcast_to(owner_row, (128, 128))
    owner_col = jnp.sum(jnp.where(i0 == i1, owner_all, 0), axis=1, keepdims=True)
    rank = jnp.sum(
        jnp.where((owner_col == owner_all) & (i0 < i1), 1, 0), axis=0, keepdims=True
    )
    pos = owner_row * 4 + rank
    pr = iota((512, 128), 0)
    place = ((pr >> 4) << 2) + (pr & 3) == pos
    for u in range(3):
        psel[u] = onehot(place & (((pr >> 2) & 3) == u))
    sel = onehot(iota((STORE, 512), 0) == (iota((STORE, 512), 1) >> 4))
    wide = mm(slot_ref[...].astype(F32).astype(BF16), sel)
    slot_row = jnp.sum(
        jnp.where(iota((4, 512), 0) == (iota((4, 512), 1) & 3), wide, 0.0), axis=0, keepdims=True
    ).astype(I32)
    col = iota((128, 512), 1)
    lands = iota((128, 512), 0) == slot_row
    for u in range(3):
        nsel[u] = onehot(lands & (((col >> 2) & 3) == u))

    right = lax.rem(y + 1, RING)
    left = lax.rem(y + RING - 1, RING)
    my_rows = pl.multiple_of(b * 128, 128)
    my_chip = pl.multiple_of(y * 256, 256)

    def chip_at(direction, dist):
        return lax.rem(y + (RING - dist if direction == 0 else dist), RING)

    def unit(chip, core, part, half):
        row = pl.multiple_of(chip * 256 + core * 128 + half * 64, 64)
        return hid.at[pl.ds(row, 64), pl.ds(part * 256, 256)]

    def ring_copy(direction, dist, part, half):
        ref = unit(chip_at(direction, dist - 1), c, part, half)
        idx = ((direction * 4 + dist - 1) * 3 + part) * 2 + half
        to = right if direction == 0 else left
        return pltpu.make_async_remote_copy(
            src_ref=ref, dst_ref=ref, send_sem=ring_send.at[idx], recv_sem=ring_recv.at[idx],
            device_id=(s, to * 2 + c), device_id_type=MESH,
        )

    def ring_arrived(direction, dist, part, half):
        ref = unit(chip_at(direction, dist), c, part, half)
        idx = ((direction * 4 + dist - 1) * 3 + part) * 2 + half
        pltpu.make_async_copy(ref, ref, ring_recv.at[idx]).wait()

    def sib_copy(direction, dist, part, half, core):
        ref = unit(chip_at(direction, dist), core, part, half)
        idx = ((direction * 4 + dist - 1) * 3 + part) * 2 + half if dist else 48 + part * 2 + half
        return pltpu.make_async_remote_copy(
            src_ref=ref, dst_ref=ref, send_sem=sib_send.at[idx], recv_sem=sib_recv.at[idx],
            device_id=(s, sib), device_id_type=MESH,
        )

    def halves(direction, dist):
        if dist < 4:
            return (0, 1)
        return (0,) if direction == 0 else (1,)

    sent = []

    def go(copy):
        copy.start()
        sent.append(copy)

    def own(part):
        bulk_wait(table.at[part, others], pull_recv.at[part])
        t = table[part].reshape(STORE * 16, 128)
        mean = mm(mix[...], t) * (1.0 / 16)
        for i in (0, 1):
            col = pl.ds(part * 256 + i * 128, 128)
            hid[pl.ds(my_rows, 128), col] = (
                nf_ref[:, col].astype(F32) + mean[i * 128 : (i + 1) * 128]
            ).astype(BF16)
        for half in (0, 1):
            for direction in (0, 1):
                go(ring_copy(direction, 1, part, half))
        for half in (0, 1):
            go(sib_copy(0, 0, part, half, c))

    def hop(dist, part):
        for half in (0, 1):
            for direction in (0, 1):
                if half not in halves(direction, dist):
                    continue
                ring_arrived(direction, dist, part, half)
                if dist < 4 and half in halves(direction, dist + 1):
                    go(ring_copy(direction, dist + 1, part, half))
                go(sib_copy(direction, dist, part, half, c))

    def wait_sib(direction, dist):
        for part in range(3):
            for half in halves(direction, dist) if dist else (0, 1):
                sib_copy(direction, dist, part, half, 1 - c).wait_recv()

    def process(chip):
        r0 = pl.multiple_of(chip * 256, 256)
        hc = hid[pl.ds(r0, 256), :]
        kc = mm(hc, wk[...]).astype(BF16)
        vt = mm_nt(wvt[pl.ds(c64, 192), :], hc).astype(BF16)
        b0 = bias_ref[pl.ds(2 * chip, 1), :]
        b1 = bias_ref[pl.ds(2 * chip + 1, 1), :]
        for h in range(HEADS_CORE):
            sc = mm_nt(kc, qm[h])
            lo = sc[0:128] + b0
            hi = sc[128:256] + b1
            top = jnp.max(jnp.maximum(lo, hi), axis=0, keepdims=True)
            old = mx_ref[h : h + 1, :]
            new = jnp.maximum(old, top)
            keep = jnp.exp(old - new)
            lo = jnp.exp(lo - new)
            hi = jnp.exp(hi - new)
            mx_ref[h : h + 1, :] = new
            mx_chip[h, pl.ds(chip, 1), :] = new
            sum_ref[h : h + 1, :] = sum_ref[h : h + 1, :] * keep + jnp.sum(lo + hi, axis=0, keepdims=True)
            pb = jnp.concatenate([lo.astype(BF16), hi.astype(BF16)], axis=0)
            p_ref[h, pl.ds(r0, 256), :] = pb
            acc_ref[h] = acc_ref[h] * keep + mm(vt[h * 64 : (h + 1) * 64], pb)

    def near(direction, dist):
        wait_sib(direction, dist)
        process(chip_at(direction, dist))

    own(0)
    own(1)
    hop(1, 0)
    own(2)
    hop(1, 1)
    hop(2, 0)
    wait_sib(0, 0)
    hc_own = hid[pl.ds(my_chip, 256), :]
    q = (mm(hc_own, wq[...]) * 0.125).astype(BF16).astype(F32)
    lq = (iota((256, 256), 1) - c * 64) >> 6
    for h in range(HEADS_CORE):
        qm[h] = jnp.where(lq == h, q, 0.0).astype(BF16)
    hop(1, 2)
    process(y)
    hop(2, 1)
    hop(3, 0)
    near(0, 1)
    hop(2, 2)
    hop(3, 1)
    near(1, 1)
    hop(4, 0)
    hop(3, 2)
    near(0, 2)
    hop(4, 1)
    near(1, 2)
    near(0, 3)
    hop(4, 2)
    gate_t[...] = mm_nt(wgt[pl.ds(c64, 192), :], hid[pl.ds(my_chip, 256), :]).astype(BF16)
    near(1, 3)
    wait_sib(0, 4)
    wait_sib(1, 4)
    process(chip_at(0, 4))

    ones = [1.0 / sum_ref[h : h + 1, :] for h in range(HEADS_CORE)]
    att = jnp.concatenate([acc_ref[h] * ones[h] for h in range(HEADS_CORE)], axis=0)
    att = att.astype(BF16).astype(F32)
    gate = gate_t[...].astype(F32)
    bg = bg_t[...].astype(F32)
    gated_t = (att * gate).astype(BF16)
    for qb in (0, 1):
        gated[qb] = gated_t[:, qb * 128 : (qb + 1) * 128]
    gated_copy = pltpu.make_async_remote_copy(
        src_ref=gated.at[1 - c], dst_ref=gsib, send_sem=gated_sems.at[0],
        recv_sem=gated_sems.at[1], device_id=(s, sib), device_id_type=MESH,
    )
    gated_copy.start()

    e0 = iota((256, 192), 0)
    tile_rows = onehot((iota((256, 192), 1) == (e0 >> 4) * 12 + (e0 & 15)) & ((e0 & 15) < 12))
    gg = mm((bg * att).astype(BF16), hid[pl.ds(my_chip, 256), :]).astype(BF16)
    gsend[...] = mm(tile_rows, gg).astype(BF16).reshape(16, 16, 768)

    def send_gate(i, _):
        to = c * 16 + lax.rem(s + i, 16)
        dest = lax.rem(s + i, 16)

        @pl.when(to == s)
        def _():
            grecv[s] = gsend[dest]

        @pl.when(to != s)
        def _():
            store_copy(gsend.at[dest], grecv.at[s], gs_sems.at[0], gs_sems.at[1], to).start()

        return 0

    lax.fori_loop(0, 16, send_gate, 0)

    back = (bg * gate).astype(BF16).astype(F32)
    backs = [back[h * 64 : (h + 1) * 64] * ones[h] for h in range(HEADS_CORE)]

    def value_part(j, total):
        r0 = pl.multiple_of(j * 256, 256)
        dv = []
        for h in range(HEADS_CORE):
            scale = jnp.exp(mx_chip[h, pl.ds(j, 1), :] - mx_ref[h : h + 1, :])
            dv.append(mm_nt((backs[h] * scale).astype(BF16), p_ref[h, pl.ds(r0, 256), :]))
        return total + mm(jnp.concatenate(dv, axis=0).astype(BF16), hid[pl.ds(r0, 256), :])

    gv = lax.fori_loop(0, RING, value_part, jnp.zeros((192, 768), F32)).astype(BF16)
    gv = mm(gv, lanes96[...]).astype(BF16)
    for j in range(RING):
        vsend[j] = gv[:, j * 128 : (j + 1) * 128]
    vrecv[y] = vsend[y]

    def send_value(k, _):
        to = lax.rem(y + k, RING)
        pltpu.make_async_remote_copy(
            src_ref=vsend.at[to], dst_ref=vrecv.at[y],
            send_sem=vy_sems.at[0], recv_sem=vy_sems.at[1],
            device_id=(s, to * 2 + c), device_id_type=MESH,
        ).start()
        return 0

    lax.fori_loop(1, RING, send_value, 0)

    gated_copy.wait_recv()
    out = nf_ref[...].astype(F32) + (
        mm_tn(gated[c], wo[pl.ds(wo_mine, 192), :]) + mm_tn(gsib[...], wo[pl.ds(wo_sib, 192), :])
    )
    out_b = out.astype(BF16)
    out_ref[...] = out_b
    pushed = mm(psel[0], out_b[:, 0:256])
    pushed = pushed + mm(psel[1], out_b[:, 256:512])
    pushed = pushed + mm(psel[2], out_b[:, 512:768])
    psend[...] = pushed.astype(BF16).reshape(STORE, 16, 256)
    send_all(psend, parr, push_sems.at[0], push_sems.at[1])
    parr[s] = psend[s]

    bulk_wait(vrecv.at[pl.ds(0, RING - 1)], vy_sems.at[1])
    total = vrecv[0].astype(F32)
    for j in range(1, RING):
        total = total + vrecv[j].astype(F32)
    tsend[...] = mm(tile_rows, total.astype(BF16)).astype(BF16).reshape(16, 16, 128)

    def send_tile(i, _):
        dest = lax.rem(s + lax.div(i, 2), 16)
        core = lax.rem(i, 2)
        to = c * 16 + dest
        own_tile = (to == s) & (core == c)

        @pl.when(own_tile)
        def _():
            tfin[s] = tsend[dest]

        @pl.when(jnp.logical_not(own_tile))
        def _():
            pltpu.make_async_remote_copy(
                src_ref=tsend.at[dest], dst_ref=tfin.at[s],
                send_sem=vs_sems.at[0], recv_sem=vs_sems.at[1],
                device_id=(to, y * 2 + core), device_id_type=MESH,
            ).start()

        return 0

    lax.fori_loop(0, 32, send_tile, 0)

    def first_tile(at_b):
        return pl.multiple_of(jnp.minimum(lax.div(at_b * 48, 128), 4) * 128, 128)

    @pl.when(in_half == c)
    def _():
        bulk_wait(grecv.at[others], gs_sems.at[1])
        sum_s = grecv[0].astype(F32)
        for j in range(1, STORE):
            sum_s = sum_s + grecv[j].astype(F32)
        hsend[...] = sum_s.astype(BF16)
        gfin[y] = hsend[:, pl.ds(first_tile(b), 256)]

        def send_rows(k, _):
            to = lax.rem(b + k, 2 * RING)
            pltpu.make_async_remote_copy(
                src_ref=hsend.at[:, pl.ds(first_tile(to), 256)], dst_ref=gfin.at[y],
                send_sem=gy_sems.at[0], recv_sem=gy_sems.at[1],
                device_id=(s, to), device_id_type=MESH,
            ).start()
            return 0

        lax.fori_loop(1, 2 * RING, send_rows, 0)

    bulk_wait(parr.at[others], push_sems.at[1])
    arrived = parr[...].reshape(STORE * 16, 256)
    for u in range(3):
        newh_ref[:, u * 256 : (u + 1) * 256] = mm(nsel[u], arrived).astype(BF16)

    def cut(x, width, offset):
        pick = onehot(
            (iota((width, 128), 0) == iota((width, 128), 1) + offset) & (iota((width, 128), 1) < 48)
        )
        high = x.astype(BF16)
        low = (x - high.astype(F32)).astype(BF16)
        return mm(high, pick) + mm(low, pick)

    @pl.when(in_half == c)
    def _():
        bulk_wait(gfin.at[pl.ds(0, RING - 1)], gy_sems.at[1])
        bulk_wait(tfin.at[others], vs_sems.at[1])

    @pl.when(in_half != c)
    def _():
        bulk_wait(gfin, gy_sems.at[1])
        bulk_wait(tfin, vs_sems.at[1])

    sum_g = gfin[0].astype(F32)
    for j in range(1, RING):
        sum_g = sum_g + gfin[j].astype(F32)
    grad_ref[0:16] = cut(sum_g, 256, b * 48 - first_tile(b))
    sum_v = tfin[0].astype(F32)
    for j in range(1, STORE):
        sum_v = sum_v + tfin[j].astype(F32)
    grad_ref[16:32] = cut(sum_v, 128, c * 48)

    bulk_wait(req_src.at[others], req_sems.at[0])
    for p in range(3):
        bulk_wait(found.at[p, others], pull_send.at[p])
    bulk_wait(psend.at[others], push_sems.at[0])
    cot_copy.wait_send()
    for copy in sent:
        copy.wait_send()
    gated_copy.wait_send()
    bulk_wait(vsend.at[pl.ds(0, RING - 1)], vy_sems.at[0])

    @pl.when(in_half == c)
    def _():
        bulk_wait(gsend.at[pl.ds(0, 15)], gs_sems.at[0])
        bulk_wait(psend.at[pl.ds(0, 15)], gy_sems.at[0])
        bulk_wait(tfin.at[others], vs_sems.at[0])

    @pl.when(in_half != c)
    def _():
        bulk_wait(gsend, gs_sems.at[0])
        bulk_wait(tfin, vs_sems.at[0])


def on_device(
    node_features, history, requests, neighbours, pattern, push_owner, push_slot,
    w_query, w_key, w_value, w_gate, w_out, cotangent,
):
    vmem = pl.BlockSpec(memory_space=pltpu.VMEM)
    hbm = pl.BlockSpec(memory_space=pltpu.HBM)
    out, newh, grads = pl.pallas_call(
        kernel,
        out_shape=(
            jax.ShapeDtypeStruct((128, 768), BF16),
            jax.ShapeDtypeStruct((128, 768), BF16),
            jax.ShapeDtypeStruct((32, 128), F32),
        ),
        in_specs=[hbm] * 13,
        out_specs=(vmem, vmem, vmem),
        scratch_shapes=[
            pltpu.VMEM((128, 768), BF16),
            pltpu.VMEM((128, 768), F32),
            pltpu.VMEM((8, STORE), I32),
            pltpu.VMEM((16, 128), I32),
            pltpu.VMEM((16, 16), I32),
            pltpu.VMEM((1, 128), I32),
            pltpu.VMEM((4, STORE), I32),
            pltpu.VMEM((768, 256), BF16),
            pltpu.VMEM((768, 256), BF16),
            pltpu.VMEM((768, 256), BF16),
            pltpu.VMEM((768, 256), BF16),
            pltpu.VMEM((384, 768), BF16),
            pltpu.VMEM((256, 768), BF16),
            pltpu.VMEM((256, 768), BF16),
            pltpu.VMEM((256, 768), BF16),
            pltpu.VMEM((STORE, 1, 128), I32),
            pltpu.VMEM((STORE, 1, 128), I32),
            pltpu.VMEM((3, STORE, 16, 128), BF16),
            pltpu.VMEM((3, STORE, 16, 128), BF16),
            pltpu.VMEM((256, 512), BF16),
            pltpu.VMEM((3, 512, 128), BF16),
            pltpu.VMEM((3, 128, 512), BF16),
            pltpu.VMEM((16, 256), F32),
            pltpu.VMEM((768, 1024), BF16),
            pltpu.VMEM((2048, 768), BF16),
            pltpu.VMEM((3, 256, 256), BF16),
            pltpu.VMEM((3, 2048, 256), BF16),
            pltpu.VMEM((3, 64, 256), F32),
            pltpu.VMEM((8, 256), F32),
            pltpu.VMEM((8, 256), F32),
            pltpu.VMEM((3, 8, 256), F32),
            pltpu.VMEM((192, 256), BF16),
            pltpu.VMEM((192, 256), BF16),
            pltpu.VMEM((2, 192, 128), BF16),
            pltpu.VMEM((192, 128), BF16),
            pltpu.VMEM((STORE, 16, 256), BF16),
            pltpu.VMEM((STORE, 16, 256), BF16),
            pltpu.VMEM((8, 192, 128), BF16),
            pltpu.VMEM((8, 192, 128), BF16),
            pltpu.VMEM((16, 16, 128), BF16),
            pltpu.VMEM((STORE, 16, 128), BF16),
            pltpu.VMEM((16, 16, 768), BF16),
            pltpu.VMEM((STORE, 16, 768), BF16),
            pltpu.VMEM((16, 768), BF16),
            pltpu.VMEM((8, 16, 256), BF16),
            pltpu.SemaphoreType.DMA((6,)),
            pltpu.SemaphoreType.DMA((7,)),
            pltpu.SemaphoreType.DMA((2,)),
            pltpu.SemaphoreType.DMA((2,)),
            pltpu.SemaphoreType.DMA((3,)),
            pltpu.SemaphoreType.DMA((3,)),
            pltpu.SemaphoreType.DMA((48,)),
            pltpu.SemaphoreType.DMA((48,)),
            pltpu.SemaphoreType.DMA((54,)),
            pltpu.SemaphoreType.DMA((54,)),
            pltpu.SemaphoreType.DMA((2,)),
            pltpu.SemaphoreType.DMA((2,)),
            pltpu.SemaphoreType.DMA((2,)),
            pltpu.SemaphoreType.DMA((2,)),
            pltpu.SemaphoreType.DMA((2,)),
            pltpu.SemaphoreType.DMA((2,)),
        ],
        compiler_params=pltpu.CompilerParams(
            collective_id=0, has_side_effects=True, vmem_limit_bytes=60 * 1024 * 1024
        ),
        cost_estimate=pl.CostEstimate(
            flops=7_000_000_000, bytes_accessed=6_000_000, transcendentals=1_600_000
        ),
    )(
        node_features, history, requests.T, neighbours.T, pattern, push_owner.reshape(1, -1),
        push_slot.T,
        cotangent, w_query, w_key, w_value, w_gate, w_out,
    )
    return (
        out,
        newh.astype(F32),
        grads[0:12, 0:48].T,
        grads[16:28, 0:48].T,
    )


def solution(mesh):
    rows = P(("storage", "batch"), None)
    in_specs = (
        rows, rows, rows, rows, P("storage", None), P(("storage", "batch")), rows,
        P(), P(), P(), P(), P(), rows,
    )
    out_specs = (rows, rows, P("batch", "storage"), P("batch", "storage"))
    return jax.shard_map(
        on_device, mesh=mesh, in_specs=in_specs, out_specs=out_specs, check_vma=False
    )
```

time: 101 us -> 84.3 us (0.83)
  local copies, waits for them, and re-layouts: 11.7 us -> 2 us
  Pallas kernels: 87.8 us -> 79.7 us
    unnamed x28 -> x3, local copies, waits for them, and re-layouts: 11 us -> 0.68 us
    pallas_call x1, Pallas kernels: 87.8 us -> 79.7 us  [on_device(): pl.pallas_call(kernel, out_shape=(jax.ShapeDtypeStruct((128, 768), BF16),...]
where the time goes in v2:
time: 84.3 us; the launch traced here: 84 us
  Pallas kernels  79.7 us (95%)
  local copies, waits for them, and re-layouts  2 us (2%)
  other arithmetic  1.74 us (2%)
    pallas_call x1, Pallas kernels, on_device(): pl.pallas_call(kernel, out_shape=(jax.ShapeDtypeStruct((128, 768), BF16),...  79.7 us
    convert_element_type x1, other arithmetic, on_device(): return (out, newh.astype(F32), grads[0:12, 0:48].T, grads[16:28, 0:48].T)  1.74 us

profile of v2, /device:TPU:1, one launch (start us, length us, event | category | flops | bytes accessed | tf_op | source)
XLA Modules:
  0.0 84.0 jit_solution(9357624710942740802)
XLA Ops:
  0.6 79.7 %shard_map.156 = (bf16[128,768]{1,0:T(8,128)(2,1)}, bf16[128,768]{1,0:T(8,128)(2,1)}, f32[32,128]{1,0:T(8,128)}) custom-call(bf16[128,768]{1,0:T(8,128)(2,1)} %nf_hbm.1, f32[128,768]{1,0:T(8,128)} %hist_hbm.1, s32[8,32]{1,0:T(8,128)} %bitcast.9, s32[16,128]{1,0:T(8,128)} %bitcast.8, s32[16,16]{1,0:T(8,128)} %pat_hbm.1, s32[1,128]{1,0:T(1,128)} %bitcast.11, ...), custom_call_target="tpu_custom_call" | custom-call | flops 7000000000 | bytes 6000000 | tf_op jit(solution)/shard_map/pallas_call | solution.py:529
  80.3 1.3 %slice_bitcast_fusion = (f32[48,12]{0,1:T(8,128)}, f32[48,12]{0,1:T(8,128)}) fusion(f32[32,128]{1,0:T(8,128)} %get-tuple-element.9), kind=kLoop, calls=%fused_computation | loop fusion | bytes 9216 | tf_op jit(solution)/shard_map/transpose | solution.py:616
  81.6 0.0 copy-start
  81.6 1.7 %convert_element_type.3 = f32[128,768]{1,0:T(8,128)} convert(bf16[128,768]{1,0:T(8,128)(2,1)} %get-tuple-element.8) | non-fusion elementwise | flops 98304 | bytes 589824 | tf_op jit(solution)/shard_map/convert_element_type | solution.py:614
  83.4 0.0 copy-done
  83.4 0.7 copy.18
Async XLA Ops:
  81.6 1.7 %copy-start = (bf16[128,768]{1,0:T(8,128)(2,1)S(1)}, bf16[128,768]{1,0:T(8,128)(2,1)}, u32[]{:S(2)}) copy-start(bf16[128,768]{1,0:T(8,128)(2,1)} %get-tuple-element.16) | copy-start | bytes 589828

commit v3 on v2

--- a/solution.py
+++ b/solution.py
@@ -38,7 +38,7 @@
 def kernel(
     nf_hbm, hist_hbm, req_hbm, nbr_hbm, pat_hbm, owner_hbm, slot_hbm,
     cot_hbm, wq_hbm, wk_hbm, wv_hbm, wg_hbm, wo_hbm,
-    out_ref, newh_ref, grad_ref,
+    rows_ref, grad_ref,
     nf_ref, hist_ref, req_ref, nbr_ref, pat_ref, owner_ref, slot_ref,
     wq, wk, wv, wg, wo, wvt, wgt, cot,
     req_src, asked, found, table, mix, psel, nsel, bias_ref, lanes96,
@@ -95,42 +95,8 @@
     small[0].wait()
     eye8 = onehot(iota((8, 128), 0) == iota((8, 128), 1))
     req_src[...] = mm_tn(req_ref[...].astype(F32).astype(BF16), eye8).astype(I32).reshape(STORE, 1, 128)
-    pl.semaphore_wait(barrier, 2 * (STORE - 1) + 2 * RING - 1)
-
-    def store_copy(src, dst, send_sem, recv_sem, peer):
-        return pltpu.make_async_remote_copy(
-            src_ref=src, dst_ref=dst, send_sem=send_sem, recv_sem=recv_sem,
-            device_id=(peer, b), device_id_type=MESH,
-        )
-
-    def send_all(src, dst, send_sem, recv_sem):
-        def body(k, _):
-            peer = lax.rem(s + k, STORE)
-            store_copy(src.at[peer], dst.at[s], send_sem, recv_sem, peer).start()
-            return 0
-
-        lax.fori_loop(1, STORE, body, 0)
-
-    def bulk_wait(ref, sem):
-        pltpu.make_async_copy(ref, ref, sem).wait()
-
-    others = pl.ds(0, STORE - 1)
-
-    send_all(req_src, asked, req_sems.at[0], req_sems.at[1])
-    asked[s] = req_src[s]
-    cot_copy = pltpu.make_async_remote_copy(
-        src_ref=cot_hbm, dst_ref=cot.at[pl.ds(win, 128)],
-        send_sem=cot_sems.at[0], recv_sem=cot_sems.at[1],
-        device_id=(s, sib), device_id_type=MESH,
-    )
-    cot_copy.start()
-
     for copy in small[1:]:
         copy.wait()
-    hist_b = hist_ref[...].astype(BF16)
-    hist_l = jnp.concatenate([hist_b[:, p * 256 : p * 256 + 128] for p in range(3)], axis=1)
-    hist_r = jnp.concatenate([hist_b[:, p * 256 + 128 : p * 256 + 256] for p in range(3)], axis=1)
-    rep = onehot(iota((STORE * 16, STORE), 1) == (iota((STORE * 16, STORE), 0) >> 4))
     nbr = nbr_ref[...]
     at = iota((256, 128), 0)
     count = jnp.zeros((256, 128), F32)
@@ -143,6 +109,73 @@
     mix[0:128] = mm_tn(count, onehot(dst_i == home)).astype(BF16)
     mix[128:256] = mm_tn(count, onehot(dst_i == home + 8)).astype(BF16)
 
+    owner_row = owner_ref[...]
+    i0 = iota((128, 128), 0)
+    i1 = iota((128, 128), 1)
+    owner_all = jnp.broadcast_to(owner_row, (128, 128))
+    owner_col = jnp.sum(jnp.where(i0 == i1, owner_all, 0), axis=1, keepdims=True)
+    rank = jnp.sum(
+        jnp.where((owner_col == owner_all) & (i0 < i1), 1, 0), axis=0, keepdims=True
+    )
+    pos = owner_row * 4 + rank
+    pr = iota((512, 128), 0)
+    place = ((pr >> 4) << 2) + (pr & 3) == pos
+    for u in range(3):
+        psel[u] = onehot(place & (((pr >> 2) & 3) == u))
+    sel = onehot(iota((STORE, 512), 0) == (iota((STORE, 512), 1) >> 4))
+    wide = mm(slot_ref[...].astype(F32).astype(BF16), sel)
+    slot_row = jnp.sum(
+        jnp.where(iota((4, 512), 0) == (iota((4, 512), 1) & 3), wide, 0.0), axis=0, keepdims=True
+    ).astype(I32)
+    col = iota((128, 512), 1)
+    lands = iota((128, 512), 0) == slot_row
+    for u in range(3):
+        nsel[u] = onehot(lands & (((col >> 2) & 3) == u))
+
+    qsel = onehot(iota((16, 256), 0) == 2 * y + (iota((16, 256), 1) >> 7))
+    seen = mm_tn(pat_ref[...].astype(F32).astype(BF16), qsel)
+    bias_ref[...] = (seen - 1.0) * NEG
+    mx_ref[...] = jnp.full_like(mx_ref, -2.0 * NEG)
+    sum_ref[...] = jnp.zeros_like(sum_ref)
+    acc_ref[...] = jnp.zeros_like(acc_ref)
+    pl.semaphore_wait(barrier, 2 * (STORE - 1) + 2 * RING - 1)
+
+    def store_copy(src, dst, send_sem, recv_sem, peer):
+        return pltpu.make_async_remote_copy(
+            src_ref=src, dst_ref=dst, send_sem=send_sem, recv_sem=recv_sem,
+            device_id=(peer, b), device_id_type=MESH,
+        )
+
+    def send_all(src, dst, send_sem, recv_sem):
+        def body(k, _):
+            peer = lax.rem(s + k, STORE)
+            store_copy(src.at[peer], dst.at[s], send_sem, recv_sem, peer).start()
+            return 0
+
+        lax.fori_loop(1, STORE, body, 0)
+
+    def bulk_wait(ref, sem):
+        pltpu.make_async_copy(ref, ref, sem).wait()
+
+    others = pl.ds(0, STORE - 1)
+
+    send_all(req_src, asked, req_sems.at[0], req_sems.at[1])
+    asked[s] = req_src[s]
+    cot_copy = pltpu.make_async_remote_copy(
+        src_ref=cot_hbm, dst_ref=cot.at[pl.ds(win, 128)],
+        send_sem=cot_sems.at[0], recv_sem=cot_sems.at[1],
+        device_id=(s, sib), device_id_type=MESH,
+    )
+    cot_copy.start()
+
+    hist_b = hist_ref[...].astype(BF16)
+    hist_l = jnp.concatenate([hist_b[:, p * 256 : p * 256 + 128] for p in range(3)], axis=1)
+    hist_r = jnp.concatenate([hist_b[:, p * 256 + 128 : p * 256 + 256] for p in range(3)], axis=1)
+    rep = onehot(iota((STORE * 16, STORE), 1) == (iota((STORE * 16, STORE), 0) >> 4))
+    for copy in loads:
+        copy.wait()
+    wvt[...] = wv[...].T
+    wgt[...] = wg[...].T
     bulk_wait(asked.at[others], req_sems.at[1])
 
     asked_f = asked[...].reshape(STORE, 128).astype(F32).astype(BF16)
@@ -161,47 +194,14 @@
     for p in range(3):
         table[p, s] = found[p, s]
 
-    for copy in loads:
-        copy.wait()
-    wvt[...] = wv[...].T
-    wgt[...] = wg[...].T
-    qsel = onehot(iota((16, 256), 0) == 2 * y + (iota((16, 256), 1) >> 7))
-    seen = mm_tn(pat_ref[...].astype(F32).astype(BF16), qsel)
-    bias_ref[...] = (seen - 1.0) * NEG
-    mx_ref[...] = jnp.full_like(mx_ref, -2.0 * NEG)
-    sum_ref[...] = jnp.zeros_like(sum_ref)
-    acc_ref[...] = jnp.zeros_like(acc_ref)
+    lr = iota((768, 1024), 0)
+    ll = iota((768, 1024), 1)
+    lanes96[...] = onehot((lr == (ll >> 7) * 96 + (ll & 127)) & ((ll & 127) < 96))
+
     cot_copy.wait_recv()
     wo_mine = pl.multiple_of(c * 192, 64)
     wo_sib = pl.multiple_of((1 - c) * 192, 64)
     bg_t[...] = mm_nt(wo[pl.ds(wo_mine, 192), :], cot[...]).astype(BF16)
-
-    lr = iota((768, 1024), 0)
-    ll = iota((768, 1024), 1)
-    lanes96[...] = onehot((lr == (ll >> 7) * 96 + (ll & 127)) & ((ll & 127) < 96))
-
-    owner_row = owner_ref[...]
-    i0 = iota((128, 128), 0)
-    i1 = iota((128, 128), 1)
-    owner_all = jnp.broadcast_to(owner_row, (128, 128))
-    owner_col = jnp.sum(jnp.where(i0 == i1, owner_all, 0), axis=1, keepdims=True)
-    rank = jnp.sum(
-        jnp.where((owner_col == owner_all) & (i0 < i1), 1, 0), axis=0, keepdims=True
-    )
-    pos = owner_row * 4 + rank
-    pr = iota((512, 128), 0)
-    place = ((pr >> 4) << 2) + (pr & 3) == pos
-    for u in range(3):
-        psel[u] = onehot(place & (((pr >> 2) & 3) == u))
-    sel = onehot(iota((STORE, 512), 0) == (iota((STORE, 512), 1) >> 4))
-    wide = mm(slot_ref[...].astype(F32).astype(BF16), sel)
-    slot_row = jnp.sum(
-        jnp.where(iota((4, 512), 0) == (iota((4, 512), 1) & 3), wide, 0.0), axis=0, keepdims=True
-    ).astype(I32)
-    col = iota((128, 512), 1)
-    lands = iota((128, 512), 0) == slot_row
-    for u in range(3):
-        nsel[u] = onehot(lands & (((col >> 2) & 3) == u))
 
     right = lax.rem(y + 1, RING)
     left = lax.rem(y + RING - 1, RING)
@@ -386,9 +386,16 @@
         return total + mm(jnp.concatenate(dv, axis=0).astype(BF16), hid[pl.ds(r0, 256), :])
 
     gv = lax.fori_loop(0, RING, value_part, jnp.zeros((192, 768), F32)).astype(BF16)
-    gv = mm(gv, lanes96[...]).astype(BF16)
+    gv = mm(gv, lanes96[...])
+    tail = jnp.concatenate([gv[144:192, j * 128 : (j + 1) * 128] for j in range(RING)], axis=0)
+    tail = tail.astype(BF16)
+    lead = iota((128, 128), 0)
+    free = iota((128, 128), 1)
+    moves = [onehot((free - 96 + 32 * k == lead) & (free >= 96)) for k in range(3)]
+    moved = [mm(tail, moves[k]) for k in range(3)]
     for j in range(RING):
-        vsend[j] = gv[:, j * 128 : (j + 1) * 128]
+        extra = jnp.concatenate([m[j * 48 : (j + 1) * 48] for m in moved], axis=0)
+        vsend[j] = (gv[0:144, j * 128 : (j + 1) * 128] + extra).astype(BF16)
     vrecv[y] = vsend[y]
 
     def send_value(k, _):
@@ -407,7 +414,7 @@
         mm_tn(gated[c], wo[pl.ds(wo_mine, 192), :]) + mm_tn(gsib[...], wo[pl.ds(wo_sib, 192), :])
     )
     out_b = out.astype(BF16)
-    out_ref[...] = out_b
+    rows_ref[0] = out_b
     pushed = mm(psel[0], out_b[:, 0:256])
     pushed = pushed + mm(psel[1], out_b[:, 256:512])
     pushed = pushed + mm(psel[2], out_b[:, 512:768])
@@ -415,11 +422,26 @@
     send_all(psend, parr, push_sems.at[0], push_sems.at[1])
     parr[s] = psend[s]
 
+    bulk_wait(req_src.at[others], req_sems.at[0])
+    for p in range(3):
+        bulk_wait(found.at[p, others], pull_send.at[p])
+    cot_copy.wait_send()
+    for copy in sent:
+        copy.wait_send()
+    gated_copy.wait_send()
+
     bulk_wait(vrecv.at[pl.ds(0, RING - 1)], vy_sems.at[1])
     total = vrecv[0].astype(F32)
     for j in range(1, RING):
         total = total + vrecv[j].astype(F32)
-    tsend[...] = mm(tile_rows, total.astype(BF16)).astype(BF16).reshape(16, 16, 128)
+    total = total.astype(BF16)
+    rest = mm_nt(total[0:48], moves[0]) + mm_nt(total[48:96], moves[1]) + mm_nt(total[96:144], moves[2])
+    t0 = iota((256, 144), 0)
+    rows_a = onehot((iota((256, 144), 1) == (t0 >> 4) * 12 + (t0 & 15)) & ((t0 & 15) < 12))
+    t1 = iota((256, 48), 0)
+    rows_b = onehot((iota((256, 48), 1) + 144 == (t1 >> 4) * 12 + (t1 & 15)) & ((t1 & 15) < 12))
+    tiles = mm(rows_a, total) + mm(rows_b, rest.astype(BF16))
+    tsend[...] = tiles.astype(BF16).reshape(16, 16, 128)
 
     def send_tile(i, _):
         dest = lax.rem(s + lax.div(i, 2), 16)
@@ -469,7 +491,7 @@
     bulk_wait(parr.at[others], push_sems.at[1])
     arrived = parr[...].reshape(STORE * 16, 256)
     for u in range(3):
-        newh_ref[:, u * 256 : (u + 1) * 256] = mm(nsel[u], arrived).astype(BF16)
+        rows_ref[1, :, u * 256 : (u + 1) * 256] = mm(nsel[u], arrived).astype(BF16)
 
     def cut(x, width, offset):
         pick = onehot(
@@ -482,31 +504,31 @@
     @pl.when(in_half == c)
     def _():
         bulk_wait(gfin.at[pl.ds(0, RING - 1)], gy_sems.at[1])
-        bulk_wait(tfin.at[others], vs_sems.at[1])
 
     @pl.when(in_half != c)
     def _():
         bulk_wait(gfin, gy_sems.at[1])
-        bulk_wait(tfin, vs_sems.at[1])
 
     sum_g = gfin[0].astype(F32)
     for j in range(1, RING):
         sum_g = sum_g + gfin[j].astype(F32)
     grad_ref[0:16] = cut(sum_g, 256, b * 48 - first_tile(b))
+
+    @pl.when(in_half == c)
+    def _():
+        bulk_wait(tfin.at[others], vs_sems.at[1])
+
+    @pl.when(in_half != c)
+    def _():
+        bulk_wait(tfin, vs_sems.at[1])
+
     sum_v = tfin[0].astype(F32)
     for j in range(1, STORE):
         sum_v = sum_v + tfin[j].astype(F32)
     grad_ref[16:32] = cut(sum_v, 128, c * 48)
 
-    bulk_wait(req_src.at[others], req_sems.at[0])
-    for p in range(3):
-        bulk_wait(found.at[p, others], pull_send.at[p])
+    bulk_wait(vsend.at[pl.ds(0, RING - 1)], vy_sems.at[0])
     bulk_wait(psend.at[others], push_sems.at[0])
-    cot_copy.wait_send()
-    for copy in sent:
-        copy.wait_send()
-    gated_copy.wait_send()
-    bulk_wait(vsend.at[pl.ds(0, RING - 1)], vy_sems.at[0])
 
     @pl.when(in_half == c)
     def _():
@@ -526,15 +548,14 @@
 ):
     vmem = pl.BlockSpec(memory_space=pltpu.VMEM)
     hbm = pl.BlockSpec(memory_space=pltpu.HBM)
-    out, newh, grads = pl.pallas_call(
+    both, grads = pl.pallas_call(
         kernel,
         out_shape=(
-            jax.ShapeDtypeStruct((128, 768), BF16),
-            jax.ShapeDtypeStruct((128, 768), BF16),
-            jax.ShapeDtypeStruct((32, 128), F32),
+            pltpu.VMEM((2, 128, 768), BF16),
+            pltpu.VMEM((32, 128), F32),
         ),
         in_specs=[hbm] * 13,
-        out_specs=(vmem, vmem, vmem),
+        out_specs=(vmem, vmem),
         scratch_shapes=[
             pltpu.VMEM((128, 768), BF16),
             pltpu.VMEM((128, 768), F32),
@@ -573,8 +594,8 @@
             pltpu.VMEM((192, 128), BF16),
             pltpu.VMEM((STORE, 16, 256), BF16),
             pltpu.VMEM((STORE, 16, 256), BF16),
-            pltpu.VMEM((8, 192, 128), BF16),
-            pltpu.VMEM((8, 192, 128), BF16),
+            pltpu.VMEM((8, 144, 128), BF16),
+            pltpu.VMEM((8, 144, 128), BF16),
             pltpu.VMEM((16, 16, 128), BF16),
             pltpu.VMEM((STORE, 16, 128), BF16),
             pltpu.VMEM((16, 16, 768), BF16),
@@ -610,8 +631,8 @@
         cotangent, w_query, w_key, w_value, w_gate, w_out,
     )
     return (
-        out,
-        newh.astype(F32),
+        both[0],
+        both[1].astype(F32),
         grads[0:12, 0:48].T,
         grads[16:28, 0:48].T,
     )

time: 84.3 us -> 79.8 us (0.947)
  Pallas kernels: 79.7 us -> 77.5 us
  local copies, waits for them, and re-layouts: 2 us -> 0.61 us
  other arithmetic: 1.74 us -> 0.84 us
    pallas_call x1, Pallas kernels: 79.7 us -> 77.5 us  [on_device(): pl.pallas_call(kernel, out_shape=(pltpu.VMEM((2, 128, 768), BF16), pltpu....]
    convert_element_type x1, other arithmetic: 1.74 us -> 0.84 us  [on_device(): both[1].astype(F32)]
where the time goes in v3:
time: 79.8 us; the launch traced here: 79.6 us
  Pallas kernels  77.5 us (97%)
  other arithmetic  0.84 us (1%)
    pallas_call x1, Pallas kernels, on_device(): pl.pallas_call(kernel, out_shape=(pltpu.VMEM((2, 128, 768), BF16), pltpu....  77.5 us

profile of v3, /device:TPU:1, one launch (start us, length us, event | category | flops | bytes accessed | tf_op | source)
XLA Modules:
  0.0 79.6 jit_solution(220519920661441080)
XLA Ops:
  0.6 77.5 %shard_map.156 = (bf16[2,128,768]{2,1,0:T(8,128)(2,1)S(1)}, f32[32,128]{1,0:T(8,128)S(1)}) custom-call(bf16[128,768]{1,0:T(8,128)(2,1)} %nf_hbm.1, f32[128,768]{1,0:T(8,128)} %hist_hbm.1, s32[8,32]{1,0:T(8,128)} %bitcast.14, s32[16,128]{1,0:T(8,128)} %bitcast.13, s32[16,16]{1,0:T(8,128)} %pat_hbm.1, s32[1,128]{1,0:T(1,128)} %bitcast.16, s32[4,32]{1,0:T(4,128)} %bitcast.15, ...), custom_call_target="tpu_custom_call" | custom-call | flops 7000000000 | bytes 6000000 | tf_op jit(solution)/shard_map/pallas_call | solution.py:551
  78.2 0.6 slice_bitcast_fusion.1
  78.8 0.8 %bitcast_convert_fusion = (f32[128,768]{1,0:T(8,128)}, bf16[128,768]{1,0:T(8,128)(2,1)}) fusion(bf16[2,128,768]{2,1,0:T(8,128)(2,1)S(1)} %get-tuple-element.6), kind=kLoop, calls=%fused_computation | loop fusion | flops 98304 | bytes 983040 | tf_op jit(solution)/shard_map/convert_element_type | solution.py:635

commit v4 on v3

--- a/solution.py
+++ b/solution.py
@@ -41,9 +41,10 @@
     rows_ref, grad_ref,
     nf_ref, hist_ref, req_ref, nbr_ref, pat_ref, owner_ref, slot_ref,
     wq, wk, wv, wg, wo, wvt, wgt, cot,
-    req_src, asked, found, table, mix, psel, nsel, bias_ref, lanes96,
+    req_src, asked, found, table, mix, psel, nsel, bias_ref,
     hid, qm, p_ref, acc_ref, mx_ref, sum_ref, mx_chip, gate_t, bg_t,
     gated, gsib, psend, parr, vsend, vrecv, tsend, tfin, gsend, grecv, hsend, gfin,
+    tile_rows, rows_a, rows_b, moves,
     load_sem, small_sem, cot_sems, req_sems, pull_send, pull_recv,
     ring_send, ring_recv, sib_send, sib_recv,
     gated_sems, push_sems, vy_sems, vs_sems, gs_sems, gy_sems,
@@ -169,8 +170,6 @@
     cot_copy.start()
 
     hist_b = hist_ref[...].astype(BF16)
-    hist_l = jnp.concatenate([hist_b[:, p * 256 : p * 256 + 128] for p in range(3)], axis=1)
-    hist_r = jnp.concatenate([hist_b[:, p * 256 + 128 : p * 256 + 256] for p in range(3)], axis=1)
     rep = onehot(iota((STORE * 16, STORE), 1) == (iota((STORE * 16, STORE), 0) >> 4))
     for copy in loads:
         copy.wait()
@@ -186,18 +185,29 @@
     hit = mine == lane
     pick_l = onehot(hit & ((prow & 8) == 0))
     pick_r = onehot(hit & ((prow & 8) != 0))
-    rows = (mm(pick_l, hist_l) + mm(pick_r, hist_r)).astype(BF16)
     for p in range(3):
-        found[p] = rows[:, p * 128 : (p + 1) * 128].reshape(STORE, 16, 128)
-    for p in range(3):
+        rows = mm(pick_l, hist_b[:, p * 256 : p * 256 + 128])
+        rows = rows + mm(pick_r, hist_b[:, p * 256 + 128 : p * 256 + 256])
+        found[p] = rows.astype(BF16).reshape(STORE, 16, 128)
         send_all(found.at[p], table.at[p], pull_send.at[p], pull_recv.at[p])
     for p in range(3):
         table[p, s] = found[p, s]
 
-    lr = iota((768, 1024), 0)
-    ll = iota((768, 1024), 1)
-    lanes96[...] = onehot((lr == (ll >> 7) * 96 + (ll & 127)) & ((ll & 127) < 96))
-
+
+    e0 = iota((256, 192), 0)
+    tile_rows[...] = onehot((iota((256, 192), 1) == (e0 >> 4) * 12 + (e0 & 15)) & ((e0 & 15) < 12))
+    lead = iota((128, 128), 0)
+    free = iota((128, 128), 1)
+    for k in range(3):
+        moves[k] = onehot((free - 96 + 32 * k == lead) & (free >= 96))
+    t0 = iota((256, 144), 0)
+    r0 = iota((256, 144), 1)
+    col_a = r0 + jnp.where(r0 >= 48, 16, 0) + jnp.where(r0 >= 96, 16, 0)
+    rows_a[...] = onehot((col_a == (t0 >> 4) * 12 + (t0 & 15)) & ((t0 & 15) < 12))
+    t1 = iota((256, 48), 0)
+    r1 = iota((256, 48), 1)
+    col_b = (r1 >> 4) * 64 + 48 + (r1 & 15)
+    rows_b[...] = onehot((col_b == (t1 >> 4) * 12 + (t1 & 15)) & ((t1 & 15) < 12))
     cot_copy.wait_recv()
     wo_mine = pl.multiple_of(c * 192, 64)
     wo_sib = pl.multiple_of((1 - c) * 192, 64)
@@ -320,6 +330,7 @@
         qm[h] = jnp.where(lq == h, q, 0.0).astype(BF16)
     hop(1, 2)
     process(y)
+    gate_t[...] = mm_nt(wgt[pl.ds(c64, 192), :], hid[pl.ds(my_chip, 256), :]).astype(BF16)
     hop(2, 1)
     hop(3, 0)
     near(0, 1)
@@ -333,7 +344,6 @@
     near(1, 2)
     near(0, 3)
     hop(4, 2)
-    gate_t[...] = mm_nt(wgt[pl.ds(c64, 192), :], hid[pl.ds(my_chip, 256), :]).astype(BF16)
     near(1, 3)
     wait_sib(0, 4)
     wait_sib(1, 4)
@@ -353,10 +363,8 @@
     )
     gated_copy.start()
 
-    e0 = iota((256, 192), 0)
-    tile_rows = onehot((iota((256, 192), 1) == (e0 >> 4) * 12 + (e0 & 15)) & ((e0 & 15) < 12))
     gg = mm((bg * att).astype(BF16), hid[pl.ds(my_chip, 256), :]).astype(BF16)
-    gsend[...] = mm(tile_rows, gg).astype(BF16).reshape(16, 16, 768)
+    gsend[...] = mm(tile_rows[...], gg).astype(BF16).reshape(16, 16, 768)
 
     def send_gate(i, _):
         to = c * 16 + lax.rem(s + i, 16)
@@ -377,37 +385,32 @@
     back = (bg * gate).astype(BF16).astype(F32)
     backs = [back[h * 64 : (h + 1) * 64] * ones[h] for h in range(HEADS_CORE)]
 
-    def value_part(j, total):
-        r0 = pl.multiple_of(j * 256, 256)
-        dv = []
-        for h in range(HEADS_CORE):
+    for h in range(HEADS_CORE):
+
+        def value_part(j, total):
+            r0 = pl.multiple_of(j * 256, 256)
             scale = jnp.exp(mx_chip[h, pl.ds(j, 1), :] - mx_ref[h : h + 1, :])
-            dv.append(mm_nt((backs[h] * scale).astype(BF16), p_ref[h, pl.ds(r0, 256), :]))
-        return total + mm(jnp.concatenate(dv, axis=0).astype(BF16), hid[pl.ds(r0, 256), :])
-
-    gv = lax.fori_loop(0, RING, value_part, jnp.zeros((192, 768), F32)).astype(BF16)
-    gv = mm(gv, lanes96[...])
-    tail = jnp.concatenate([gv[144:192, j * 128 : (j + 1) * 128] for j in range(RING)], axis=0)
-    tail = tail.astype(BF16)
-    lead = iota((128, 128), 0)
-    free = iota((128, 128), 1)
-    moves = [onehot((free - 96 + 32 * k == lead) & (free >= 96)) for k in range(3)]
-    moved = [mm(tail, moves[k]) for k in range(3)]
-    for j in range(RING):
-        extra = jnp.concatenate([m[j * 48 : (j + 1) * 48] for m in moved], axis=0)
-        vsend[j] = (gv[0:144, j * 128 : (j + 1) * 128] + extra).astype(BF16)
-    vrecv[y] = vsend[y]
-
-    def send_value(k, _):
-        to = lax.rem(y + k, RING)
-        pltpu.make_async_remote_copy(
-            src_ref=vsend.at[to], dst_ref=vrecv.at[y],
-            send_sem=vy_sems.at[0], recv_sem=vy_sems.at[1],
-            device_id=(s, to * 2 + c), device_id_type=MESH,
-        ).start()
-        return 0
-
-    lax.fori_loop(1, RING, send_value, 0)
+            dv = mm_nt((backs[h] * scale).astype(BF16), p_ref[h, pl.ds(r0, 256), :])
+            return total + mm(dv.astype(BF16), hid[pl.ds(r0, 256), :])
+
+        gv = lax.fori_loop(0, RING, value_part, jnp.zeros((64, 768), F32))
+        for j in range(RING):
+            chunk = gv[:, j * 96 : (j + 1) * 96]
+            tail = jnp.concatenate([chunk[48:64, 32 * k : 32 * k + 32] for k in range(3)], axis=0)
+            packed = jnp.concatenate([chunk[0:48], tail], axis=1)
+            vsend[j, h * 48 : (h + 1) * 48] = packed.astype(BF16)
+        vrecv[y, h * 48 : (h + 1) * 48] = vsend[y, h * 48 : (h + 1) * 48]
+
+        def send_value(k, _):
+            to = lax.rem(y + k, RING)
+            pltpu.make_async_remote_copy(
+                src_ref=vsend.at[to, pl.ds(h * 48, 48)], dst_ref=vrecv.at[y, pl.ds(h * 48, 48)],
+                send_sem=vy_sems.at[0], recv_sem=vy_sems.at[1],
+                device_id=(s, to * 2 + c), device_id_type=MESH,
+            ).start()
+            return 0
+
+        lax.fori_loop(1, RING, send_value, 0)
 
     gated_copy.wait_recv()
     out = nf_ref[...].astype(F32) + (
@@ -435,12 +438,11 @@
     for j in range(1, RING):
         total = total + vrecv[j].astype(F32)
     total = total.astype(BF16)
-    rest = mm_nt(total[0:48], moves[0]) + mm_nt(total[48:96], moves[1]) + mm_nt(total[96:144], moves[2])
-    t0 = iota((256, 144), 0)
-    rows_a = onehot((iota((256, 144), 1) == (t0 >> 4) * 12 + (t0 & 15)) & ((t0 & 15) < 12))
-    t1 = iota((256, 48), 0)
-    rows_b = onehot((iota((256, 48), 1) + 144 == (t1 >> 4) * 12 + (t1 & 15)) & ((t1 & 15) < 12))
-    tiles = mm(rows_a, total) + mm(rows_b, rest.astype(BF16))
+    rest = jnp.zeros((48, 128), F32)
+    for k in range(3):
+        part = [total[h * 48 + k * 16 : h * 48 + k * 16 + 16] for h in range(HEADS_CORE)]
+        rest = rest + mm_nt(jnp.concatenate(part, axis=0), moves[k])
+    tiles = mm(rows_a[...], total) + mm(rows_b[...], rest.astype(BF16))
     tsend[...] = tiles.astype(BF16).reshape(16, 16, 128)
 
     def send_tile(i, _):
@@ -525,7 +527,7 @@
     sum_v = tfin[0].astype(F32)
     for j in range(1, STORE):
         sum_v = sum_v + tfin[j].astype(F32)
-    grad_ref[16:32] = cut(sum_v, 128, c * 48)
+    grad_ref[16:32, 0:48] = jnp.where(c == 0, sum_v[:, 0:48], sum_v[:, 48:96])
 
     bulk_wait(vsend.at[pl.ds(0, RING - 1)], vy_sems.at[0])
     bulk_wait(psend.at[others], push_sems.at[0])
@@ -580,7 +582,6 @@
             pltpu.VMEM((3, 512, 128), BF16),
             pltpu.VMEM((3, 128, 512), BF16),
             pltpu.VMEM((16, 256), F32),
-            pltpu.VMEM((768, 1024), BF16),
             pltpu.VMEM((2048, 768), BF16),
             pltpu.VMEM((3, 256, 256), BF16),
             pltpu.VMEM((3, 2048, 256), BF16),
@@ -602,6 +603,10 @@
             pltpu.VMEM((STORE, 16, 768), BF16),
             pltpu.VMEM((16, 768), BF16),
             pltpu.VMEM((8, 16, 256), BF16),
+            pltpu.VMEM((256, 192), BF16),
+            pltpu.VMEM((256, 144), BF16),
+            pltpu.VMEM((256, 48), BF16),
+            pltpu.VMEM((3, 128, 128), BF16),
             pltpu.SemaphoreType.DMA((6,)),
             pltpu.SemaphoreType.DMA((7,)),
             pltpu.SemaphoreType.DMA((2,)),

time: 79.8 us -> 82.2 us (1.030)
  Pallas kernels: 77.5 us -> 79.9 us
    pallas_call x1, Pallas kernels: 77.5 us -> 79.9 us  [on_device(): pl.pallas_call(kernel, out_shape=(pltpu.VMEM((2, 128, 768), BF16), pltpu....]
where the time goes in v4:
time: 82.2 us; the launch traced here: 82 us
  Pallas kernels  79.9 us (97%)
  other arithmetic  0.84 us (1%)
    pallas_call x1, Pallas kernels, on_device(): pl.pallas_call(kernel, out_shape=(pltpu.VMEM((2, 128, 768), BF16), pltpu....  79.9 us

profile of v4, /device:TPU:1, one launch (start us, length us, event | category | flops | bytes accessed | tf_op | source)
XLA Modules:
  0.0 82.0 jit_solution(2251762723746614290)
XLA Ops:
  0.6 79.9 %shard_map.156 = (bf16[2,128,768]{2,1,0:T(8,128)(2,1)S(1)}, f32[32,128]{1,0:T(8,128)S(1)}) custom-call(bf16[128,768]{1,0:T(8,128)(2,1)} %nf_hbm.1, f32[128,768]{1,0:T(8,128)} %hist_hbm.1, s32[8,32]{1,0:T(8,128)} %bitcast.14, s32[16,128]{1,0:T(8,128)} %bitcast.13, s32[16,16]{1,0:T(8,128)} %pat_hbm.1, s32[1,128]{1,0:T(1,128)} %bitcast.16, s32[4,32]{1,0:T(4,128)} %bitcast.15, ...), custom_call_target="tpu_custom_call" | custom-call | flops 7000000000 | bytes 6000000 | tf_op jit(solution)/shard_map/pallas_call | solution.py:553
  80.6 0.6 slice_bitcast_fusion.1
  81.2 0.8 %bitcast_convert_fusion = (f32[128,768]{1,0:T(8,128)}, bf16[128,768]{1,0:T(8,128)(2,1)}) fusion(bf16[2,128,768]{2,1,0:T(8,128)(2,1)S(1)} %get-tuple-element.6), kind=kLoop, calls=%fused_computation | loop fusion | flops 98304 | bytes 983040 | tf_op jit(solution)/shard_map/convert_element_type | solution.py:640

commit v5 on v4

--- a/solution.py
+++ b/solution.py
@@ -44,7 +44,7 @@
     req_src, asked, found, table, mix, psel, nsel, bias_ref,
     hid, qm, p_ref, acc_ref, mx_ref, sum_ref, mx_chip, gate_t, bg_t,
     gated, gsib, psend, parr, vsend, vrecv, tsend, tfin, gsend, grecv, hsend, gfin,
-    tile_rows, rows_a, rows_b, moves,
+    tile_rows, rows_a, rows_b, moves, dvt,
     load_sem, small_sem, cot_sems, req_sems, pull_send, pull_recv,
     ring_send, ring_recv, sib_send, sib_recv,
     gated_sems, push_sems, vy_sems, vs_sems, gs_sems, gy_sems,
@@ -193,7 +193,6 @@
     for p in range(3):
         table[p, s] = found[p, s]
 
-
     e0 = iota((256, 192), 0)
     tile_rows[...] = onehot((iota((256, 192), 1) == (e0 >> 4) * 12 + (e0 & 15)) & ((e0 & 15) < 12))
     lead = iota((128, 128), 0)
@@ -201,13 +200,9 @@
     for k in range(3):
         moves[k] = onehot((free - 96 + 32 * k == lead) & (free >= 96))
     t0 = iota((256, 144), 0)
-    r0 = iota((256, 144), 1)
-    col_a = r0 + jnp.where(r0 >= 48, 16, 0) + jnp.where(r0 >= 96, 16, 0)
-    rows_a[...] = onehot((col_a == (t0 >> 4) * 12 + (t0 & 15)) & ((t0 & 15) < 12))
+    rows_a[...] = onehot((iota((256, 144), 1) == (t0 >> 4) * 12 + (t0 & 15)) & ((t0 & 15) < 12))
     t1 = iota((256, 48), 0)
-    r1 = iota((256, 48), 1)
-    col_b = (r1 >> 4) * 64 + 48 + (r1 & 15)
-    rows_b[...] = onehot((col_b == (t1 >> 4) * 12 + (t1 & 15)) & ((t1 & 15) < 12))
+    rows_b[...] = onehot((iota((256, 48), 1) + 144 == (t1 >> 4) * 12 + (t1 & 15)) & ((t1 & 15) < 12))
     cot_copy.wait_recv()
     wo_mine = pl.multiple_of(c * 192, 64)
     wo_sib = pl.multiple_of((1 - c) * 192, 64)
@@ -385,32 +380,29 @@
     back = (bg * gate).astype(BF16).astype(F32)
     backs = [back[h * 64 : (h + 1) * 64] * ones[h] for h in range(HEADS_CORE)]
 
-    for h in range(HEADS_CORE):
-
-        def value_part(j, total):
-            r0 = pl.multiple_of(j * 256, 256)
-            scale = jnp.exp(mx_chip[h, pl.ds(j, 1), :] - mx_ref[h : h + 1, :])
-            dv = mm_nt((backs[h] * scale).astype(BF16), p_ref[h, pl.ds(r0, 256), :])
-            return total + mm(dv.astype(BF16), hid[pl.ds(r0, 256), :])
-
-        gv = lax.fori_loop(0, RING, value_part, jnp.zeros((64, 768), F32))
-        for j in range(RING):
-            chunk = gv[:, j * 96 : (j + 1) * 96]
-            tail = jnp.concatenate([chunk[48:64, 32 * k : 32 * k + 32] for k in range(3)], axis=0)
-            packed = jnp.concatenate([chunk[0:48], tail], axis=1)
-            vsend[j, h * 48 : (h + 1) * 48] = packed.astype(BF16)
-        vrecv[y, h * 48 : (h + 1) * 48] = vsend[y, h * 48 : (h + 1) * 48]
-
-        def send_value(k, _):
-            to = lax.rem(y + k, RING)
-            pltpu.make_async_remote_copy(
-                src_ref=vsend.at[to, pl.ds(h * 48, 48)], dst_ref=vrecv.at[y, pl.ds(h * 48, 48)],
-                send_sem=vy_sems.at[0], recv_sem=vy_sems.at[1],
-                device_id=(s, to * 2 + c), device_id_type=MESH,
-            ).start()
-            return 0
-
-        lax.fori_loop(1, RING, send_value, 0)
+    for j in range(RING):
+        dv = []
+        for h in range(HEADS_CORE):
+            scale = jnp.exp(mx_chip[h, j : j + 1, :] - mx_ref[h : h + 1, :])
+            dv.append(mm_nt((backs[h] * scale).astype(BF16), p_ref[h, j * 256 : (j + 1) * 256, :]))
+        dvt[:, j * 256 : (j + 1) * 256] = jnp.concatenate(dv, axis=0).astype(BF16)
+    gv = mm(dvt[...], hid[...])
+    for j in range(RING):
+        chunk = gv[:, j * 96 : (j + 1) * 96]
+        tail = jnp.concatenate([chunk[144:192, 32 * k : 32 * k + 32] for k in range(3)], axis=0)
+        vsend[j] = jnp.concatenate([chunk[0:144], tail], axis=1).astype(BF16)
+    vrecv[y] = vsend[y]
+
+    def send_value(k, _):
+        to = lax.rem(y + k, RING)
+        pltpu.make_async_remote_copy(
+            src_ref=vsend.at[to], dst_ref=vrecv.at[y],
+            send_sem=vy_sems.at[0], recv_sem=vy_sems.at[1],
+            device_id=(s, to * 2 + c), device_id_type=MESH,
+        ).start()
+        return 0
+
+    lax.fori_loop(1, RING, send_value, 0)
 
     gated_copy.wait_recv()
     out = nf_ref[...].astype(F32) + (
@@ -438,10 +430,7 @@
     for j in range(1, RING):
         total = total + vrecv[j].astype(F32)
     total = total.astype(BF16)
-    rest = jnp.zeros((48, 128), F32)
-    for k in range(3):
-        part = [total[h * 48 + k * 16 : h * 48 + k * 16 + 16] for h in range(HEADS_CORE)]
-        rest = rest + mm_nt(jnp.concatenate(part, axis=0), moves[k])
+    rest = mm_nt(total[0:48], moves[0]) + mm_nt(total[48:96], moves[1]) + mm_nt(total[96:144], moves[2])
     tiles = mm(rows_a[...], total) + mm(rows_b[...], rest.astype(BF16))
     tsend[...] = tiles.astype(BF16).reshape(16, 16, 128)
 
@@ -607,6 +596,7 @@
             pltpu.VMEM((256, 144), BF16),
             pltpu.VMEM((256, 48), BF16),
             pltpu.VMEM((3, 128, 128), BF16),
+            pltpu.VMEM((192, 2048), BF16),
             pltpu.SemaphoreType.DMA((6,)),
             pltpu.SemaphoreType.DMA((7,)),
             pltpu.SemaphoreType.DMA((2,)),

time: 82.2 us -> 79.3 us (0.965)
  Pallas kernels: 79.9 us -> 77 us
    pallas_call x1, Pallas kernels: 79.9 us -> 77 us  [on_device(): pl.pallas_call(kernel, out_shape=(pltpu.VMEM((2, 128, 768), BF16), pltpu....]
where the time goes in v5:
time: 79.3 us; the launch traced here: 79.1 us
  Pallas kernels  77 us (97%)
  other arithmetic  0.84 us (1%)
    pallas_call x1, Pallas kernels, on_device(): pl.pallas_call(kernel, out_shape=(pltpu.VMEM((2, 128, 768), BF16), pltpu....  77 us

profile of v5, /device:TPU:1, one launch (start us, length us, event | category | flops | bytes accessed | tf_op | source)
XLA Modules:
  0.0 79.1 jit_solution(6664755450788690338)
XLA Ops:
  0.6 77.0 %shard_map.156 = (bf16[2,128,768]{2,1,0:T(8,128)(2,1)S(1)}, f32[32,128]{1,0:T(8,128)S(1)}) custom-call(bf16[128,768]{1,0:T(8,128)(2,1)} %nf_hbm.1, f32[128,768]{1,0:T(8,128)} %hist_hbm.1, s32[8,32]{1,0:T(8,128)} %bitcast.14, s32[16,128]{1,0:T(8,128)} %bitcast.13, s32[16,16]{1,0:T(8,128)} %pat_hbm.1, s32[1,128]{1,0:T(1,128)} %bitcast.16, s32[4,32]{1,0:T(4,128)} %bitcast.15, ...), custom_call_target="tpu_custom_call" | custom-call | flops 7000000000 | bytes 6000000 | tf_op jit(solution)/shard_map/pallas_call | solution.py:542
  77.7 0.6 slice_bitcast_fusion.1
  78.3 0.8 %bitcast_convert_fusion = (f32[128,768]{1,0:T(8,128)}, bf16[128,768]{1,0:T(8,128)(2,1)}) fusion(bf16[2,128,768]{2,1,0:T(8,128)(2,1)S(1)} %get-tuple-element.6), kind=kLoop, calls=%fused_computation | loop fusion | flops 98304 | bytes 983040 | tf_op jit(solution)/shard_map/convert_element_type | solution.py:630

commit v6 on v5

--- a/solution.py
+++ b/solution.py
@@ -44,7 +44,7 @@
     req_src, asked, found, table, mix, psel, nsel, bias_ref,
     hid, qm, p_ref, acc_ref, mx_ref, sum_ref, mx_chip, gate_t, bg_t,
     gated, gsib, psend, parr, vsend, vrecv, tsend, tfin, gsend, grecv, hsend, gfin,
-    tile_rows, rows_a, rows_b, moves, dvt,
+    tile_rows, rows_a, rows_b, moves, dvt, odd_rows, unpack,
     load_sem, small_sem, cot_sems, req_sems, pull_send, pull_recv,
     ring_send, ring_recv, sib_send, sib_recv,
     gated_sems, push_sems, vy_sems, vs_sems, gs_sems, gy_sems,
@@ -195,6 +195,13 @@
 
     e0 = iota((256, 192), 0)
     tile_rows[...] = onehot((iota((256, 192), 1) == (e0 >> 4) * 12 + (e0 & 15)) & ((e0 & 15) < 12))
+    e2 = iota((128, 192), 0)
+    odd_rows[...] = onehot((iota((128, 192), 1) == (e2 >> 3) * 12 + (e2 & 7) + 4) & ((e2 & 7) >= 4))
+    ut = iota((16, 80), 0)
+    ur = iota((16, 80), 1)
+    for u in range(6):
+        far = 48 + (u // 2) * 8 + (u % 2) * 4 - 8
+        unpack[u] = onehot((ur == ut + jnp.where(ut < 8, u * 8, far)) & (ut < 12))
     lead = iota((128, 128), 0)
     free = iota((128, 128), 1)
     for k in range(3):
@@ -359,7 +366,15 @@
     gated_copy.start()
 
     gg = mm((bg * att).astype(BF16), hid[pl.ds(my_chip, 256), :]).astype(BF16)
-    gsend[...] = mm(tile_rows[...], gg).astype(BF16).reshape(16, 16, 768)
+    ga = mm(tile_rows[...], gg)
+    gb = mm(odd_rows[...], gg)
+    for i in range(16):
+        packed = [ga[i * 16 : i * 16 + 8, u * 128 : (u + 1) * 128] for u in range(6)]
+        for u in range(0, 6, 2):
+            even = ga[i * 16 + 8 : i * 16 + 16, u * 128 : (u + 1) * 128]
+            packed.append(even + gb[i * 8 : i * 8 + 8, (u + 1) * 128 : (u + 2) * 128])
+        packed.append(jnp.zeros((8, 128), F32))
+        gsend[i] = jnp.concatenate(packed, axis=0).astype(BF16)
 
     def send_gate(i, _):
         to = c * 16 + lax.rem(s + i, 16)
@@ -414,6 +429,14 @@
     pushed = pushed + mm(psel[1], out_b[:, 256:512])
     pushed = pushed + mm(psel[2], out_b[:, 512:768])
     psend[...] = pushed.astype(BF16).reshape(STORE, 16, 256)
+    @pl.when(in_half == c)
+    def _():
+        bulk_wait(gsend.at[pl.ds(0, 15)], gs_sems.at[0])
+
+    @pl.when(in_half != c)
+    def _():
+        bulk_wait(gsend, gs_sems.at[0])
+
     send_all(psend, parr, push_sems.at[0], push_sems.at[1])
     parr[s] = psend[s]
 
@@ -465,7 +488,9 @@
         sum_s = grecv[0].astype(F32)
         for j in range(1, STORE):
             sum_s = sum_s + grecv[j].astype(F32)
-        hsend[...] = sum_s.astype(BF16)
+        sum_s = sum_s.astype(BF16)
+        for u in range(6):
+            hsend[:, u * 128 : (u + 1) * 128] = mm(unpack[u], sum_s).astype(BF16)
         gfin[y] = hsend[:, pl.ds(first_tile(b), 256)]
 
         def send_rows(k, _):
@@ -523,13 +548,11 @@
 
     @pl.when(in_half == c)
     def _():
-        bulk_wait(gsend.at[pl.ds(0, 15)], gs_sems.at[0])
         bulk_wait(psend.at[pl.ds(0, 15)], gy_sems.at[0])
         bulk_wait(tfin.at[others], vs_sems.at[0])
 
     @pl.when(in_half != c)
     def _():
-        bulk_wait(gsend, gs_sems.at[0])
         bulk_wait(tfin, vs_sems.at[0])
 
 
@@ -588,8 +611,8 @@
             pltpu.VMEM((8, 144, 128), BF16),
             pltpu.VMEM((16, 16, 128), BF16),
             pltpu.VMEM((STORE, 16, 128), BF16),
-            pltpu.VMEM((16, 16, 768), BF16),
-            pltpu.VMEM((STORE, 16, 768), BF16),
+            pltpu.VMEM((16, 80, 128), BF16),
+            pltpu.VMEM((STORE, 80, 128), BF16),
             pltpu.VMEM((16, 768), BF16),
             pltpu.VMEM((8, 16, 256), BF16),
             pltpu.VMEM((256, 192), BF16),
@@ -597,6 +620,8 @@
             pltpu.VMEM((256, 48), BF16),
             pltpu.VMEM((3, 128, 128), BF16),
             pltpu.VMEM((192, 2048), BF16),
+            pltpu.VMEM((128, 192), BF16),
+            pltpu.VMEM((6, 16, 80), BF16),
             pltpu.SemaphoreType.DMA((6,)),
             pltpu.SemaphoreType.DMA((7,)),
             pltpu.SemaphoreType.DMA((2,)),

time: 79.3 us -> 77.9 us (0.982)
  Pallas kernels: 77 us -> 75.7 us
    pallas_call x1, Pallas kernels: 77 us -> 75.7 us  [on_device(): pl.pallas_call(kernel, out_shape=(pltpu.VMEM((2, 128, 768), BF16), pltpu....]
where the time goes in v6:
time: 77.9 us; the launch traced here: 77.8 us
  Pallas kernels  75.7 us (97%)
  other arithmetic  0.84 us (1%)
    pallas_call x1, Pallas kernels, on_device(): pl.pallas_call(kernel, out_shape=(pltpu.VMEM((2, 128, 768), BF16), pltpu....  75.7 us

profile of v6, /device:TPU:1, one launch (start us, length us, event | category | flops | bytes accessed | tf_op | source)
XLA Modules:
  0.0 77.8 jit_solution(10358300567237192117)
XLA Ops:
  0.6 75.7 %shard_map.156 = (bf16[2,128,768]{2,1,0:T(8,128)(2,1)S(1)}, f32[32,128]{1,0:T(8,128)S(1)}) custom-call(bf16[128,768]{1,0:T(8,128)(2,1)} %nf_hbm.1, f32[128,768]{1,0:T(8,128)} %hist_hbm.1, s32[8,32]{1,0:T(8,128)} %bitcast.14, s32[16,128]{1,0:T(8,128)} %bitcast.13, s32[16,16]{1,0:T(8,128)} %pat_hbm.1, s32[1,128]{1,0:T(1,128)} %bitcast.16, s32[4,32]{1,0:T(4,128)} %bitcast.15, ...), custom_call_target="tpu_custom_call" | custom-call | flops 7000000000 | bytes 6000000 | tf_op jit(solution)/shard_map/pallas_call | solution.py:565
  76.3 0.6 slice_bitcast_fusion.1
  76.9 0.8 %bitcast_convert_fusion = (f32[128,768]{1,0:T(8,128)}, bf16[128,768]{1,0:T(8,128)(2,1)}) fusion(bf16[2,128,768]{2,1,0:T(8,128)(2,1)S(1)} %get-tuple-element.6), kind=kLoop, calls=%fused_computation | loop fusion | flops 98304 | bytes 983040 | tf_op jit(solution)/shard_map/convert_element_type | solution.py:655

commit v7 on v6

--- a/solution.py
+++ b/solution.py
@@ -141,6 +141,15 @@
     acc_ref[...] = jnp.zeros_like(acc_ref)
     pl.semaphore_wait(barrier, 2 * (STORE - 1) + 2 * RING - 1)
 
+    def swing(i, mid):
+        return mid + lax.div(i + 1, 2) * (1 - 2 * lax.rem(i, 2))
+
+    my_x = lax.div(s, 8)
+    my_z = lax.rem(s, 8)
+
+    def far_z(i):
+        return lax.rem(my_z + swing(i, 4), 8)
+
     def store_copy(src, dst, send_sem, recv_sem, peer):
         return pltpu.make_async_remote_copy(
             src_ref=src, dst_ref=dst, send_sem=send_sem, recv_sem=recv_sem,
@@ -148,12 +157,12 @@
         )
 
     def send_all(src, dst, send_sem, recv_sem):
-        def body(k, _):
-            peer = lax.rem(s + k, STORE)
+        def body(n, _):
+            peer = lax.rem(my_x + swing(lax.rem(n, 4), 2), 4) * 8 + far_z(lax.div(n, 4))
             store_copy(src.at[peer], dst.at[s], send_sem, recv_sem, peer).start()
             return 0
 
-        lax.fori_loop(1, STORE, body, 0)
+        lax.fori_loop(0, STORE - 1, body, 0)
 
     def bulk_wait(ref, sem):
         pltpu.make_async_copy(ref, ref, sem).wait()
@@ -377,8 +386,8 @@
         gsend[i] = jnp.concatenate(packed, axis=0).astype(BF16)
 
     def send_gate(i, _):
-        to = c * 16 + lax.rem(s + i, 16)
-        dest = lax.rem(s + i, 16)
+        dest = lax.rem(i, 2) * 8 + far_z(lax.div(i, 2))
+        to = c * 16 + dest
 
         @pl.when(to == s)
         def _():
@@ -409,7 +418,7 @@
     vrecv[y] = vsend[y]
 
     def send_value(k, _):
-        to = lax.rem(y + k, RING)
+        to = lax.rem(y + swing(k, 4), RING)
         pltpu.make_async_remote_copy(
             src_ref=vsend.at[to], dst_ref=vrecv.at[y],
             send_sem=vy_sems.at[0], recv_sem=vy_sems.at[1],
@@ -417,7 +426,7 @@
         ).start()
         return 0
 
-    lax.fori_loop(1, RING, send_value, 0)
+    lax.fori_loop(0, RING - 1, send_value, 0)
 
     gated_copy.wait_recv()
     out = nf_ref[...].astype(F32) + (
@@ -458,8 +467,8 @@
     tsend[...] = tiles.astype(BF16).reshape(16, 16, 128)
 
     def send_tile(i, _):
-        dest = lax.rem(s + lax.div(i, 2), 16)
         core = lax.rem(i, 2)
+        dest = lax.rem(lax.div(i, 2), 2) * 8 + far_z(lax.div(i, 4))
         to = c * 16 + dest
         own_tile = (to == s) & (core == c)
 

time: 77.9 us -> 77.4 us (level)
  no operation moved by 1% of the time
where the time goes in v7:
time: 77.4 us; the launch traced here: 77.3 us
  Pallas kernels  75.2 us (97%)
  other arithmetic  0.84 us (1%)
    pallas_call x1, Pallas kernels, on_device(): pl.pallas_call(kernel, out_shape=(pltpu.VMEM((2, 128, 768), BF16), pltpu....  75.2 us

profile of v7, /device:TPU:1, one launch (start us, length us, event | category | flops | bytes accessed | tf_op | source)
XLA Modules:
  0.0 77.3 jit_solution(14465655741949363742)
XLA Ops:
  0.6 75.2 %shard_map.156 = (bf16[2,128,768]{2,1,0:T(8,128)(2,1)S(1)}, f32[32,128]{1,0:T(8,128)S(1)}) custom-call(bf16[128,768]{1,0:T(8,128)(2,1)} %nf_hbm.1, f32[128,768]{1,0:T(8,128)} %hist_hbm.1, s32[8,32]{1,0:T(8,128)} %bitcast.14, s32[16,128]{1,0:T(8,128)} %bitcast.13, s32[16,16]{1,0:T(8,128)} %pat_hbm.1, s32[1,128]{1,0:T(1,128)} %bitcast.16, s32[4,32]{1,0:T(4,128)} %bitcast.15, ...), custom_call_target="tpu_custom_call" | custom-call | flops 7000000000 | bytes 6000000 | tf_op jit(solution)/shard_map/pallas_call | solution.py:574
  75.8 0.6 slice_bitcast_fusion.1
  76.5 0.8 %bitcast_convert_fusion = (f32[128,768]{1,0:T(8,128)}, bf16[128,768]{1,0:T(8,128)(2,1)}) fusion(bf16[2,128,768]{2,1,0:T(8,128)(2,1)S(1)} %get-tuple-element.6), kind=kLoop, calls=%fused_computation | loop fusion | flops 98304 | bytes 983040 | tf_op jit(solution)/shard_map/convert_element_type | solution.py:664

commit v8 on v7

--- a/solution.py
+++ b/solution.py
@@ -349,13 +349,13 @@
     hop(3, 1)
     near(1, 1)
     hop(4, 0)
+    near(0, 2)
     hop(3, 2)
-    near(0, 2)
+    near(1, 2)
     hop(4, 1)
-    near(1, 2)
     near(0, 3)
+    near(1, 3)
     hop(4, 2)
-    near(1, 3)
     wait_sib(0, 4)
     wait_sib(1, 4)
     process(chip_at(0, 4))

time: 77.4 us -> 77.6 us (level)
  no operation moved by 1% of the time
where the time goes in v8:
time: 77.6 us; the launch traced here: 77.4 us
  Pallas kernels  75.3 us (97%)
  other arithmetic  0.84 us (1%)
    pallas_call x1, Pallas kernels, on_device(): pl.pallas_call(kernel, out_shape=(pltpu.VMEM((2, 128, 768), BF16), pltpu....  75.3 us

profile of v8, /device:TPU:1, one launch (start us, length us, event | category | flops | bytes accessed | tf_op | source)
XLA Modules:
  0.0 77.4 jit_solution(11506782378118566464)
XLA Ops:
  0.6 75.3 %shard_map.156 = (bf16[2,128,768]{2,1,0:T(8,128)(2,1)S(1)}, f32[32,128]{1,0:T(8,128)S(1)}) custom-call(bf16[128,768]{1,0:T(8,128)(2,1)} %nf_hbm.1, f32[128,768]{1,0:T(8,128)} %hist_hbm.1, s32[8,32]{1,0:T(8,128)} %bitcast.14, s32[16,128]{1,0:T(8,128)} %bitcast.13, s32[16,16]{1,0:T(8,128)} %pat_hbm.1, s32[1,128]{1,0:T(1,128)} %bitcast.16, s32[4,32]{1,0:T(4,128)} %bitcast.15, ...), custom_call_target="tpu_custom_call" | custom-call | flops 7000000000 | bytes 6000000 | tf_op jit(solution)/shard_map/pallas_call | solution.py:574
  76.0 0.6 slice_bitcast_fusion.1
  76.6 0.8 %bitcast_convert_fusion = (f32[128,768]{1,0:T(8,128)}, bf16[128,768]{1,0:T(8,128)(2,1)}) fusion(bf16[2,128,768]{2,1,0:T(8,128)(2,1)S(1)} %get-tuple-element.6), kind=kLoop, calls=%fused_computation | loop fusion | flops 98304 | bytes 983040 | tf_op jit(solution)/shard_map/convert_element_type | solution.py:664
